TPU v7x, 32 devices: a whole 2x2x4 slice. The times are simulated.
32 devices in a mesh: seq: 16 (over z, x, core), head: 2 (over y).
Axes of the slice: x: 2, y: 2, z: 4, core: 2. Of those that a mesh axis runs over, the one named last changes fastest.
Arguments:
- queries: bfloat16 [16384, 1024], P('seq', 'head'), may hold values from -8 to 8
- keys: bfloat16 [16384, 1024], P('seq', 'head'), may hold values from -6 to 6
- values: bfloat16 [16384, 1024], P('seq', 'head'), may hold values from -6 to 6
- partners: int32 [256, 3], P('seq'), may hold values from 0 to 255, as said below
- out_weight: bfloat16 [1024, 1024], P('head'), may hold values from -0.1875 to 0.1875
- grad_out: bfloat16 [16384, 1024], P(('seq', 'head')), may hold values from -6 to 6
Outputs:
- mixed: bfloat16 [16384, 1024], P(('seq', 'head'))
- grad_queries: bfloat16 [16384, 1024], P('seq', 'head')
- grad_keys: bfloat16 [16384, 1024], P('seq', 'head')
- grad_values: bfloat16 [16384, 1024], P('seq', 'head')
- grad_weight: float32 [1024, 1024], P('head', 'seq')
Inputs may be any that keep to these rules, and one draw needn't show every extreme that they name: `partners`: the 16 query blocks of one shard (rows 16 * d to 16 * d + 15) name at most 3 partner blocks, counted with repeats, among the blocks of any one shard (blocks 16 * s to 16 * s + 15); some pair of shards reaches 3 in every draw.
All inputs are finite; a program needn't handle non-finite values.
Results may differ from a plain program's by a relative error of at most 0.012.
The roundings to bfloat16 on the way count: a program that leaves them out, or rounds other values in their place, can miss the bound.
Values may be sent and summed in bfloat16 or wider, within the bound.
A program may use at most 192 MiB of HBM per device.

v0:
```python
import jax
import jax.numpy as jnp
from jax import lax
from jax.sharding import PartitionSpec as P

DH = 64
BLK = 64
R = 3
SUMR = 16


def with_halo(x, sides, width):
    for axis, dim in sides:
        peers, length = (lax.axis_size(axis), x.shape[dim])
        up = [(i, (i + 1) % peers) for i in range(peers - 1)]
        down = [(j, i) for i, j in up]
        last = lax.slice_in_dim(x, length - width, length, axis=dim)
        leading = lax.slice_in_dim(x, 0, width, axis=dim)
        before = lax.ppermute(last, axis, up)
        after = lax.ppermute(leading, axis, down)
        x = jnp.concatenate([before, x, after], axis=dim)
    return x


def from_behind(value, axis, steps):
    count = lax.axis_size(axis)
    leading, last = (max(0, -steps), min(count, count - steps))
    return lax.ppermute(value, axis, [(source, source + steps) for source in range(leading, last)])


def to_heads(tensor):
    first, second, width = tensor.shape
    return tensor.reshape(first, second, width // DH, DH).transpose(2, 0, 1, 3)


def from_heads(tensor):
    count, first, second, head_size = tensor.shape
    return tensor.transpose(1, 2, 0, 3).reshape(first, second, count * head_size)


def probabilities(query_per_head, key_sequence, key_digest, allowed, score_scale):
    neighbour_blocks = (
        jnp.einsum("gnm,gtm->gnt", query_per_head, key_sequence, preferred_element_type=jnp.float32)
        * score_scale
    )
    block_digest = (
        jnp.einsum("mfp,jp->mfj", query_per_head, key_digest, preferred_element_type=jnp.float32)
        * score_scale
    )
    neighbour_blocks = jnp.where(allowed[:, None, :], neighbour_blocks, -1e30)
    highest = jnp.maximum(jnp.max(neighbour_blocks, -1), jnp.max(block_digest, -1))[..., None]
    near_exp = jnp.exp(neighbour_blocks - highest)
    far_exp = jnp.exp(block_digest - highest)
    totals = (jnp.sum(near_exp, -1) + jnp.sum(far_exp, -1))[..., None]
    return (near_exp / totals, far_exp / totals)


def per_device(queries, keys, values, partners, out_weight, grad_out):
    shards = lax.axis_size("seq")
    my_shard = lax.axis_index("seq")
    tokens = queries.shape[0]
    blocks = tokens // BLK
    width_local = queries.shape[1]
    score_scale = DH ** (-0.5)
    capacity = (R * blocks + shards - 1) // shards
    requests = blocks * R
    kv_pair = jnp.stack([keys, values], 0)
    padded = with_halo(kv_pair, (("seq", 1),), BLK)
    padded = padded.reshape(2, blocks + 2, BLK, width_local)
    window = jnp.concatenate([padded[:, :-2], padded[:, 1:-1], padded[:, 2:]], 2)
    wanted = partners.reshape(-1)
    owners = wanted // blocks
    inside = wanted % blocks
    request_order = jnp.arange(requests)
    earlier = (owners[:, None] == owners[None, :]) & (
        request_order[None, :] < request_order[:, None]
    )
    ranks = jnp.sum(earlier.astype(jnp.int32), 1)
    slots = owners * capacity + ranks
    slot_hits = (slots[:, None] == jnp.arange(shards * capacity)[None, :]).astype(jnp.int32)
    asks = (jnp.sum(slot_hits * (inside[:, None] + 1), 0) - 1).reshape(shards, capacity)
    asked = lax.all_to_all(asks, "seq", split_axis=0, concat_axis=0, tiled=True)
    asked_flat = asked.reshape(-1)
    own_blocks = kv_pair.reshape(2, blocks, BLK, width_local)
    outgoing = jnp.take(own_blocks, jnp.maximum(asked_flat, 0), axis=1)
    outgoing = jnp.where((asked_flat >= 0)[None, :, None, None], outgoing, jnp.zeros_like(outgoing))
    outgoing = outgoing.reshape(2, shards, capacity, BLK, width_local)
    arrived = lax.all_to_all(outgoing, "seq", split_axis=1, concat_axis=1, tiled=True)
    chosen = jnp.take(arrived.reshape(2, shards * capacity, BLK, width_local), slots, axis=1)
    chosen = chosen.reshape(2, blocks, R * BLK, width_local)
    key_sequence = jnp.concatenate([window[0], chosen[0]], 1)
    value_sequence = jnp.concatenate([window[1], chosen[1]], 1)
    block_digest = lax.all_gather(own_blocks[:, 0, :SUMR], "seq", axis=1, tiled=True)
    global_ids = my_shard * blocks + jnp.arange(blocks)
    left_ok = jnp.broadcast_to((global_ids > 0)[:, None], (blocks, BLK))
    right_ok = jnp.broadcast_to((global_ids < blocks * shards - 1)[:, None], (blocks, BLK))
    allowed = jnp.concatenate(
        [left_ok, jnp.ones((blocks, BLK), bool), right_ok, jnp.ones((blocks, R * BLK), bool)], 1
    )
    query_heads = to_heads(queries.reshape(blocks, BLK, width_local))
    key_heads = to_heads(key_sequence)
    value_heads = to_heads(value_sequence)
    sum_keys = to_heads(block_digest[0][None])[:, 0]
    sum_values = to_heads(block_digest[1][None])[:, 0]

    def attend(parts):
        head_queries, head_keys, head_values, digest_key_head, digest_value_head = parts
        local_probs, distant_probs = probabilities(
            head_queries, head_keys, digest_key_head, allowed, score_scale
        )
        result = jnp.einsum(
            "teh,thz->tez",
            local_probs.astype(jnp.bfloat16),
            head_values,
            preferred_element_type=jnp.float32,
        )
        result = result + jnp.einsum(
            "umj,jc->umc",
            distant_probs.astype(jnp.bfloat16),
            digest_value_head,
            preferred_element_type=jnp.float32,
        )
        return result.astype(jnp.bfloat16)

    attended_heads = lax.map(attend, (query_heads, key_heads, value_heads, sum_keys, sum_values))
    attended = from_heads(attended_heads).reshape(tokens, width_local)
    mixed = lax.psum_scatter(
        jnp.dot(attended, out_weight, preferred_element_type=jnp.float32).astype(jnp.bfloat16),
        "head",
        scatter_dimension=0,
        tiled=True,
    )
    grad_full = lax.all_gather(grad_out, "head", axis=0, tiled=True)
    grad_attended = lax.dot_general(
        grad_full, out_weight, (((1,), (1,)), ((), ())), preferred_element_type=jnp.float32
    ).astype(jnp.bfloat16)
    weight_terms = lax.dot_general(
        attended, grad_full, (((0,), (0,)), ((), ())), preferred_element_type=jnp.float32
    )
    grad_weight = lax.psum_scatter(weight_terms, "seq", scatter_dimension=1, tiled=True)
    grad_heads = to_heads(grad_attended.reshape(blocks, BLK, width_local))

    def differentiate(parts):
        (
            head_queries,
            head_keys,
            head_values,
            digest_key_head,
            digest_value_head,
            gradient_head,
            a_head,
        ) = parts
        local_probs, distant_probs = probabilities(
            head_queries, head_keys, digest_key_head, allowed, score_scale
        )
        local_bias = local_probs.astype(jnp.bfloat16)
        distant_bias = distant_probs.astype(jnp.bfloat16)
        local_prob_grad = jnp.einsum(
            "gnm,gtm->gnt", gradient_head, head_values, preferred_element_type=jnp.float32
        )
        distant_prob_grad = jnp.einsum(
            "mfp,jp->mfj", gradient_head, digest_value_head, preferred_element_type=jnp.float32
        )
        offset = jnp.sum(gradient_head.astype(jnp.float32) * a_head.astype(jnp.float32), -1)[
            ..., None
        ]
        local_score_grad = (local_probs * (local_prob_grad - offset) * score_scale).astype(
            jnp.bfloat16
        )
        distant_score_grad = (distant_probs * (distant_prob_grad - offset) * score_scale).astype(
            jnp.bfloat16
        )
        query_gradient = jnp.einsum(
            "teh,thz->tez", local_score_grad, head_keys, preferred_element_type=jnp.float32
        )
        query_gradient = (
            query_gradient
            + jnp.einsum(
                "umj,jc->umc",
                distant_score_grad,
                digest_key_head,
                preferred_element_type=jnp.float32,
            )
        ).astype(jnp.bfloat16)
        local_key_grad = jnp.einsum(
            "sfv,sfz->svz", local_score_grad, head_queries, preferred_element_type=jnp.float32
        )
        local_value_grad = jnp.einsum(
            "sfv,sfz->svz", local_bias, gradient_head, preferred_element_type=jnp.float32
        )
        distant_key_grad = jnp.einsum(
            "ngm,ngz->mz", distant_score_grad, head_queries, preferred_element_type=jnp.float32
        )
        distant_value_grad = jnp.einsum(
            "ngm,ngz->mz", distant_bias, gradient_head, preferred_element_type=jnp.float32
        )
        return (
            query_gradient,
            local_key_grad,
            local_value_grad,
            distant_key_grad,
            distant_value_grad,
        )

    results = lax.map(
        differentiate,
        (query_heads, key_heads, value_heads, sum_keys, sum_values, grad_heads, attended_heads),
    )
    grad_queries = from_heads(results[0]).reshape(tokens, width_local)
    nearby_terms = jnp.stack([from_heads(results[1]), from_heads(results[2])], 0)
    summary_terms = jnp.stack(
        [from_heads(results[3][:, None])[0], from_heads(results[4][:, None])[0]], 0
    )
    middle = nearby_terms[:, :, BLK : 2 * BLK]
    leftward = nearby_terms[:, :, :BLK]
    rightward = nearby_terms[:, :, 2 * BLK : 3 * BLK]
    from_next = from_behind(leftward[:, 0].astype(jnp.bfloat16), "seq", -1).astype(jnp.float32)
    from_prev = from_behind(rightward[:, -1].astype(jnp.bfloat16), "seq", 1).astype(jnp.float32)
    own_grad = middle + jnp.concatenate([leftward[:, 1:], from_next[:, None]], 1)
    own_grad = own_grad + jnp.concatenate([from_prev[:, None], rightward[:, :-1]], 1)
    partner_part = (
        nearby_terms[:, :, 3 * BLK :].reshape(2, requests, BLK, width_local).astype(jnp.bfloat16)
    )
    returning = (
        jnp.zeros((2, shards * capacity, BLK, width_local), jnp.bfloat16)
        .at[:, slots]
        .set(partner_part)
    )
    returning = returning.reshape(2, shards, capacity, BLK, width_local)
    returned = lax.all_to_all(returning, "seq", split_axis=1, concat_axis=1, tiled=True).astype(
        jnp.float32
    )
    summary_grad = lax.psum_scatter(summary_terms, "seq", scatter_dimension=1, tiled=True)
    taken = (asked_flat[:, None] == jnp.arange(blocks)[None, :]).astype(jnp.float32)
    incoming = jnp.einsum(
        "sn,csbf->cnbf",
        taken,
        returned.reshape(2, shards * capacity, BLK, width_local),
        precision=lax.Precision.HIGHEST,
    )
    own_grad = own_grad + incoming
    own_grad = own_grad.at[:, 0, :SUMR].add(summary_grad)
    grad_keys = own_grad[0].reshape(tokens, width_local).astype(jnp.bfloat16)
    grad_values = own_grad[1].reshape(tokens, width_local).astype(jnp.bfloat16)
    return (mixed, grad_queries, grad_keys, grad_values, grad_weight)


def solution(mesh):
    in_specs = (
        P("seq", "head"),
        P("seq", "head"),
        P("seq", "head"),
        P("seq", None),
        P("head", None),
        P(("seq", "head"), None),
    )
    out_specs = (
        P(("seq", "head"), None),
        P("seq", "head"),
        P("seq", "head"),
        P("seq", "head"),
        P("head", "seq"),
    )
    return jax.shard_map(
        per_device, mesh=mesh, in_specs=in_specs, out_specs=out_specs, check_vma=False
    )
```

profile of v0, /device:TPU:11, one launch (start us, length us, event | category | flops | bytes accessed | tf_op | source)
XLA Modules:
  0.0 822.7 jit_solution(12159852832203825671)
XLA Ops:
  9.6 6.6 all-to-all-start
  20.2 5.0 gather_fusion
  25.2 6.2 copy.284
  31.6 3.9 select_select_fusion
  35.5 3.2 copy.285
  38.7 7.3 all-to-all-start.1
  46.7 3.3 collective-permute-start
  52.3 143.0 %all-gather = bf16[2,1,256,512]{3,0,1,2:T(2,128)(2,1)S(1)} all-gather(bf16[2,1,16,512]{3,0,1,2:T(2,128)(2,1)S(1)} %copy.289), channel_id=2, replica_groups=mesh['seq'=16,'head'=2] {'seq'}, dimensions={2}, use_global_device_ids=true | all-gather | bytes 557056 | tf_op jit(solution)/shard_map/all_gather | solution.py:93
  204.9 4.8 pad_maximum_fusion.1
  209.7 3.1 fusion.104
  212.8 5.9 copy.291
  218.7 5.9 copy.276
  224.7 3.8 convolution_convert_fusion.1
  228.5 3.9 reshape_reshape.14
  232.4 3.5 copy.338
  235.9 6.3 copy.286
  242.2 7.8 gather_fusion.1
  250.0 3.4 select_bitcast_fusion
  253.5 3.4 fusion.105
  256.9 8.9 %concatenate.41 = bf16[16,192,8,64]{3,2,1,0:T(8,128)(2,1)} reshape(bf16[1,48,64,512]{3,2,0,1:T(8,128)(2,1)} %get-tuple-element.355) | data formatting | bytes 6291456 | tf_op jit(solution)/shard_map/concatenate | solution.py:92
  265.7 8.4 %copy.292 = bf16[16,192,8,64]{1,3,2,0:T(8,128)(2,1)} copy(bf16[16,192,8,64]{3,2,1,0:T(8,128)(2,1)} %concatenate.41) | data formatting | bytes 6291456 | tf_op jit(solution)/shard_map/concatenate | solution.py:92
  274.2 8.7 %maximum_bitcast_fusion.1 = bf16[8,16,384,64]{2,3,0,1:T(8,128)(2,1)} fusion(bf16[16,192,8,64]{1,3,2,0:T(8,128)(2,1)} %copy.292, bf16[16,192,8,64]{1,3,2,0:T(8,128)(2,1)} %bitcast.274), kind=kLoop, calls=%fused_computation.109 | loop fusion | flops 12582912 | bytes 12582912 | tf_op jit(solution)/shard_map/transpose | solution.py:33
  282.8 6.5 copy.296
  289.3 8.9 %concatenate.38 = bf16[16,192,8,64]{3,2,1,0:T(8,128)(2,1)} reshape(bf16[1,48,64,512]{3,2,0,1:T(8,128)(2,1)} %get-tuple-element.356) | data formatting | bytes 6291456 | tf_op jit(solution)/shard_map/concatenate | solution.py:91
  298.2 8.3 %copy.288 = bf16[16,192,8,64]{1,3,2,0:T(8,128)(2,1)} copy(bf16[16,192,8,64]{3,2,1,0:T(8,128)(2,1)} %concatenate.38) | data formatting | bytes 6291456 | tf_op jit(solution)/shard_map/concatenate | solution.py:91
  306.5 8.6 %maximum_bitcast_fusion = bf16[8,16,384,64]{2,3,0,1:T(8,128)(2,1)} fusion(bf16[16,192,8,64]{1,3,2,0:T(8,128)(2,1)} %copy.288, bf16[16,192,8,64]{1,3,2,0:T(8,128)(2,1)} %bitcast.273), kind=kLoop, calls=%fused_computation.108 | loop fusion | flops 12582912 | bytes 12582912 | tf_op jit(solution)/shard_map/transpose | solution.py:33
  315.0 6.5 copy.295
  323.4 52.3 %while.29 = (s32[]{:T(128)}, bf16[8,16,64,64]{3,2,1,0:T(8,128)(2,1)}, pred[16,384]{1,0:T(8,128)(4,1)S(1)}, bf16[8,16,64,64]{3,2,1,0:T(8,128)(2,1)S(1)}, bf16[8,1...) while((s32[]{:T(128)}, ...), condition=%wide.region_7.8_spmd, body=%wide.region_2.0_spmd.sunk | while | flops 172881920 | bytes 10888797 | solution.py:125
  377.5 123.1 %while.30 = (s32[]{:T(128)}, bf16[8,16,64,64]{3,2,1,0:T(8,128)(2,1)}, f32[8,16,384,64]{2,3,0,1:T(8,128)}, f32[8,16,384,64]{2,3,0,1:T(8,128)}, f32[8,256,64]{1,2,...) while((s32[]{:T(128)}, ...), condition=%wide.region_15.16_spmd, body=%wide.region_9.15_spmd.sunk | while | flops 428733440 | bytes 27643056 | solution.py:205
  500.7 12.8 %copy.305 = f32[1,16,384,512]{3,1,2,0:T(8,128)} copy(f32[1,16,384,512]{2,3,1,0:T(8,128)} %bitcast.283) | data formatting | bytes 25165824 | tf_op jit(solution)/shard_map/stack;reshape | solution.py:210
  513.5 12.7 %copy.306 = f32[1,16,384,512]{3,1,2,0:T(8,128)} copy(f32[1,16,384,512]{2,3,1,0:T(8,128)} %bitcast.284) | data formatting | bytes 25165824 | tf_op jit(solution)/shard_map/stack;reshape | solution.py:210
  526.2 9.5 %fusion.79 = bf16[2,16,384,512]{3,1,2,0:T(8,128)(2,1)S(1)} fusion(f32[1,16,384,512]{3,1,2,0:T(8,128)} %copy.306, f32[1,16,384,512]{3,1,2,0:T(8,128)} %copy.305), kind=kLoop, calls=%fused_computation.106 | loop fusion | flops 6291456 | bytes 37748736 | tf_op jit(solution)/shard_map/convert.7
  535.7 3.8 slice.150
  542.0 8.9 %copy.307 = bf16[2,16,192,512]{3,2,1,0:T(8,128)(2,1)} copy(bf16[2,16,192,512]{3,1,2,0:T(8,128)(2,1)} %slice.150) | data formatting | bytes 12582912 | tf_op jit(solution)/shard_map/slice | solution.py:222
  551.0 6.2 copy.308
  557.2 3.4 broadcast.335
  560.6 16.8 %scatter_fusion = bf16[2,48,64,512]{3,2,1,0:T(8,128)(2,1)} fusion(bf16[2,48,64,512]{3,2,1,0:T(8,128)(2,1)} %broadcast.335, s32[48]{0:T(128)S(1)} %copy-done.14, bf16[48,2,64,512]{3,2,1,0:T(8,128)(2,1)} %copy.308), kind=kCustom, calls=%fused_computation.2 | custom fusion | bytes 18874560 | tf_op jit(solution)/shard_map/scatter | solution.py:227
  577.3 6.2 copy.309
  583.5 5.9 all-to-all-start.2
  592.1 3.4 copy.297
  597.5 4.6 fusion.109
  610.5 4.3 collective-permute-start.3
  614.9 6.2 fusion.87
  624.9 109.9 %collective-permute-done.2 = bf16[2,64,512]{2,1,0:T(8,128)(2,1)S(1)} collective-permute-done((bf16[2,64,512]{2,1,0:T(8,128)(2,1)S(1)}, bf16[2,64,512]{2,1,0:T(8,128)(2,1)S(1)}, u32[]{:S(2)}, u32[]{:S(2)}) %collective-permute-start.2) | collective-permute-done | bytes 131104 | tf_op jit(solution)/shard_map/ppermute | solution.py:28
  736.0 3.9 copy.310
  741.6 7.8 fusion.85
  758.5 21.9 %reduce-scatter.8.cloned.1.call-done = f32[512,64]{0,1:T(8,128)} async-done(((f32[512,1024]{0,1:T(8,128)}), f32[512,64]{0,1:T(8,128)}) %reduce-scatter.8.cloned.1.call-update) | async-done | bytes 131088 | tf_op jit(solution)/shard_map/reduce_scatter | solution.py:140
  780.4 35.5 %reduce-scatter.4.cloned.1.call-done = bf16[512,1024]{1,0:T(8,128)(2,1)} async-done(((bf16[1024,1024]{1,0:T(8,128)(2,1)}), bf16[512,1024]{1,0:T(8,128)(2,1)}) %reduce-scatter.4.cloned.1.call-update) | async-done | bytes 1048592 | tf_op jit(solution)/shard_map/reduce_scatter | solution.py:127
  (313 shorter events, 228.2 us)
Async XLA Ops:
  7.2 217.5 %copy-start = (bf16[512,1024]{1,0:T(8,128)(2,1)S(1)}, bf16[512,1024]{1,0:T(8,128)(2,1)}, u32[]{:S(2)}) copy-start(bf16[512,1024]{1,0:T(8,128)(2,1)} %param.16) | copy-start | bytes 3145732
  9.6 10.3 %all-to-all-start = ((s32[16,1,3]{2,1,0:T(1,128)}), s32[16,1,3]{2,1,0:T(1,128)S(1)}, u32[]{:S(2)}, u32[]{:S(2)}) async-start(s32[16,1,3]{2,1,0:T(1,128)} %bitcast.29), calls=%async_computation | async-start | bytes 16384 | tf_op jit(solution)/shard_map/all_to_all | solution.py:82
  19.9 5.3 copy-start.11
  38.7 7.3 copy-start.2
  38.7 7.3 copy-start.3
  38.7 197.3 %all-to-all-start.1 = ((bf16[2,16,3,64,512]{4,3,2,0,1:T(8,128)(2,1)}), bf16[2,16,3,64,512]{4,3,2,0,1:T(8,128)(2,1)}, u32[]{:S(2)}, u32[]{:S(2)}) async-start(bf16[2,16,3,64,512]{4,3,2,0,1:T(8,128)(2,1)} %copy.285), calls=%async_computation.1 | async-start | bytes 12582912 | tf_op jit(solution)/shard_map/all_to_all | solution.py:88
  45.9 178.7 %all-gather.3.cloned.1.call-start = ((), (), s32[]{:S(2)}) async-start(), calls=%async_computation.7 | async-start | bytes 3145728 | tf_op jit(solution)/shard_map/all_gather | solution.py:133
  46.7 155.4 %collective-permute-start = (bf16[2,64,512]{2,1,0:T(8,128)(2,1)}, bf16[2,64,512]{2,1,0:T(8,128)(2,1)S(1)}, u32[]{:S(2)}, u32[]{:S(2)}) collective-permute-start(bf16[2,64,512]{2,1,0:T(8,128)(2,1)} %get-tuple-element.362), channel_id=1, source_target_pairs={{0,2},{2,4},{4,6},{6,8},{8,10},{10,12},{12,14},{14,16},{16,18},{18... | collective-permute-start | bytes 393224 | tf_op jit(solution)/shard_map/ppermute | solution.py:19
  50.1 152.1 %collective-permute-start.1 = (bf16[2,64,512]{2,1,0:T(8,128)(2,1)}, bf16[2,64,512]{2,1,0:T(8,128)(2,1)}, u32[]{:S(2)}, u32[]{:S(2)}) collective-permute-start(bf16[2,64,512]{2,1,0:T(8,128)(2,1)} %get-tuple-element.363), channel_id=1, source_target_pairs={{2,0},{4,2},{6,4},{8,6},{10,8},{12,10},{14,12},{16,14},{18,16},{20... | collective-permute-start | bytes 393224 | tf_op jit(solution)/shard_map/ppermute | solution.py:20
  52.0 145.9 %copy-start.8 = (bf16[1024,512]{1,0:T(8,128)(2,1)S(1)}, bf16[1024,512]{1,0:T(8,128)(2,1)}, u32[]{:S(2)}) copy-start(bf16[1024,512]{1,0:T(8,128)(2,1)} %param.12) | copy-start | bytes 3145732
  196.3 5.8 copy-start.13
  242.2 7.8 copy-start.15
  377.9 3.1 copy-start.7
  393.3 3.1 copy-start.7
  408.6 3.1 copy-start.7
  423.9 3.1 copy-start.7
  439.3 3.1 copy-start.7
  454.7 3.1 copy-start.7
  470.0 3.1 copy-start.7
  485.3 3.1 copy-start.7
  535.7 6.4 copy-start.1
  557.2 3.4 copy-start.14
  583.5 7.2 copy-start.10
  583.5 152.5 %all-to-all-start.2 = ((bf16[2,16,3,64,512]{4,3,2,0,1:T(8,128)(2,1)}), bf16[2,16,3,64,512]{4,3,2,0,1:T(8,128)(2,1)}, u32[]{:S(2)}, u32[]{:S(2)}) async-start(bf16[2,16,3,64,512]{4,3,2,0,1:T(8,128)(2,1)} %copy.309), calls=%async_computation.3 | async-start | bytes 12582912 | tf_op jit(solution)/shard_map/all_to_all | solution.py:230
  589.5 160.0 %reduce-scatter.6.cloned.1.call-start = ((), (), s32[]{:S(2)}) async-start(), calls=%async_computation.8 | async-start | bytes 1114112 | tf_op jit(solution)/shard_map/reduce_scatter | solution.py:233
  592.0 188.4 %reduce-scatter.8.cloned.1.call-start = ((), (), s32[]{:S(2)}) async-start(), calls=%async_computation.9 | async-start | bytes 2228224 | tf_op jit(solution)/shard_map/reduce_scatter | solution.py:140
  597.5 4.7 copy-start.9
  602.1 3.3 copy-start.12
  602.2 213.8 %reduce-scatter.4.cloned.1.call-start = ((), (), s32[]{:S(2)}) async-start(), calls=%async_computation.6 | async-start | bytes 3145728 | tf_op jit(solution)/shard_map/reduce_scatter | solution.py:127
  608.2 126.6 %collective-permute-start.2 = (bf16[2,64,512]{2,1,0:T(8,128)(2,1)S(1)}, bf16[2,64,512]{2,1,0:T(8,128)(2,1)S(1)}, u32[]{:S(2)}, u32[]{:S(2)}) collective-permute-start(bf16[2,64,512]{2,1,0:T(8,128)(2,1)S(1)} %bitcast.293), channel_id=1, source_target_pairs={{2,0},{4,2},{6,4},{8,6},{10,8},{12,10},{14,12},{16,14},{18,16},{20... | collective-permute-start | bytes 393224 | tf_op jit(solution)/shard_map/ppermute | solution.py:28
  610.5 10.6 %copy-start.6 = (bf16[8,16,64,64]{3,2,1,0:T(8,128)(2,1)S(1)}, bf16[8,16,64,64]{3,2,1,0:T(8,128)(2,1)}, u32[]{:S(2)}) copy-start(bf16[8,16,64,64]{3,2,1,0:T(8,128)(2,1)} %get-tuple-element.136) | copy-start | bytes 3145732
  610.5 124.4 %collective-permute-start.3 = (bf16[2,64,512]{2,1,0:T(8,128)(2,1)S(1)}, bf16[2,64,512]{2,1,0:T(8,128)(2,1)}, u32[]{:S(2)}, u32[]{:S(2)}) collective-permute-start(bf16[2,64,512]{2,1,0:T(8,128)(2,1)S(1)} %bitcast.294), channel_id=1, source_target_pairs={{0,2},{2,4},{4,6},{6,8},{8,10},{10,12},{12,14},{14,16},{16,18},{18... | collective-permute-start | bytes 393224 | tf_op jit(solution)/shard_map/ppermute | solution.py:28
  736.0 4.3 copy-start.4
  736.0 5.6 copy-start.5
Sparse Core Ops, SparseCore 0:
  52.1 34.0 all-gather.2
  594.5 111.4 reduce-scatter.5
  710.7 69.6 reduce-scatter.7
  783.1 32.8 reduce-scatter.3
where the time goes:
time: 834 us; the launch traced here: 823 us
  local copies, waits for them, and re-layouts  214 us (26%)
  waiting for transfers between devices  169 us (20%)
  matrix products  168 us (20%)
  blocking collectives  143 us (17%)
  other arithmetic  80.7 us (10%)
  starting transfers between devices  31.8 us (4%)
  between operations  14.4 us (2%)
    all_gather x1, blocking collectives, per_device(): lax.all_gather(own_blocks[:, 0, :SUMR], 'seq', axis=1, tiled=True)  143 us
    ppermute x2, waiting for transfers between devices, from_behind(): lax.ppermute(value, axis, [(source, source + steps) for source in range(l...  110 us
    reduce_scatter x1, waiting for transfers between devices, per_device(): lax.psum_scatter(jnp.dot(attended, out_weight, preferred_element_type=jnp...  35.5 us
    dot_general x16, matrix products, probabilities(): jnp.einsum('gnm,gtm->gnt', query_per_head, key_sequence, preferred_elemen...  26.2 us
    another operation x2, local copies, waits for them, and re-layouts, per_device(): jnp.stack([from_heads(results[1]), from_heads(results[2])], 0)  25.5 us
    reduce_scatter x1, waiting for transfers between devices, per_device(): lax.psum_scatter(weight_terms, 'seq', scatter_dimension=1, tiled=True)  21.9 us
    dot_general x8, matrix products, attend(): jnp.einsum('teh,thz->tez', local_probs.astype(jnp.bfloat16), head_values,...  18.9 us
    dot_general x8, matrix products, differentiate(): jnp.einsum('teh,thz->tez', local_score_grad, head_keys, preferred_element...  18.2 us
  transfers between devices with their start and end apart: 11, of which 4 were waited for; matrix products, arithmetic and copies ran while one was open for 11% of the time, Pallas kernels for 0%

commit v1 on v0

v1 whole, which is shorter than its diff:
```python
import functools

import jax
import jax.numpy as jnp
from jax import lax
from jax.experimental import pallas as pl
from jax.experimental.pallas import tpu as pltpu
from jax.sharding import PartitionSpec as P

DH = 64
BLK = 64
R = 3
SUMR = 16
LANES = 128
CHUNKS = 1
VMEM = 48 * 1024 * 1024
F32 = jnp.float32
BF16 = jnp.bfloat16


def pack_kernel(capacity, chunks, asked, k_ref, v_ref, *outs):
    shard = pl.program_id(0)
    width = k_ref.shape[1] // chunks
    for c, out in enumerate(outs):
        cols = slice(c * width, (c + 1) * width)
        for j, src in enumerate((k_ref, v_ref)):
            for n in range(capacity):
                block = jnp.maximum(asked[shard * capacity + n], 0)
                rows = pl.ds(pl.multiple_of(block * BLK, BLK), BLK)
                at = (j * capacity + n) * BLK
                out[0, at : at + BLK, :] = src[rows, cols]
            at = 2 * capacity * BLK + j * SUMR
            out[0, at : at + SUMR, :] = src[0:SUMR, cols]


def attend_kernel(
    capacity, meta, q_ref, k_ref, v_ref, arrived, g_ref, gft_ref,
    att_ref, dq_ref, dk_ref, dv_ref, back, kl, vl, dks, dvs,
):
    shards = arrived.shape[0]
    tokens = q_ref.shape[0]
    blocks = tokens // BLK
    requests = blocks * R
    nsum = shards * SUMR
    near = (3 + R) * BLK
    total = near + nsum
    sum_at = 2 * capacity * BLK
    weight_at = sum_at + 2 * SUMR
    weight_rows = back.shape[1] - weight_at
    first = lax.broadcasted_iota(jnp.int32, (1, LANES), 1) < DH
    place = lax.broadcasted_iota(jnp.int32, (1, total), 1)

    kl[near:, :] = arrived[:, sum_at : sum_at + SUMR, :].reshape(nsum, LANES)
    vl[near:, :] = arrived[:, sum_at + SUMR : sum_at + 2 * SUMR, :].reshape(nsum, LANES)
    dk_ref[...] = jnp.zeros_like(dk_ref)
    dv_ref[...] = jnp.zeros_like(dv_ref)
    dks[...] = jnp.zeros_like(dks)
    dvs[...] = jnp.zeros_like(dvs)

    def both(x):
        zero = jnp.zeros_like(x)
        return jnp.concatenate([jnp.where(first, x, zero), jnp.where(first, zero, x)], 0)

    def merge(x):
        return jnp.where(first, x[:BLK], x[BLK:])

    def step(i, carry):
        row = pl.multiple_of(i * BLK, BLK)
        here = pl.ds(row, BLK)
        window = pl.ds(row, 3 * BLK)
        kl[0 : 3 * BLK, :] = k_ref[window, :]
        vl[0 : 3 * BLK, :] = v_ref[window, :]
        spots = []
        for r in range(R):
            owner = meta[i * R + r]
            rank = meta[requests + i * R + r]
            at_k = pl.ds(pl.multiple_of(rank * BLK, BLK), BLK)
            at_v = pl.ds(pl.multiple_of((capacity + rank) * BLK, BLK), BLK)
            spots.append((owner, at_k, at_v))
            at = (3 + r) * BLK
            kl[at : at + BLK, :] = arrived[owner, at_k, :]
            vl[at : at + BLK, :] = arrived[owner, at_v, :]
        keys = kl[...]
        vals = vl[...]
        qs = both(q_ref[here, :] * jnp.asarray(DH**-0.5, BF16))
        g = g_ref[here, :]
        gs = both(g)
        nt = (((1,), (1,)), ((), ()))
        tn = (((0,), (0,)), ((), ()))
        s = lax.dot_general(qs, keys, nt, preferred_element_type=F32)
        no_left = (i == 0) & (meta[2 * requests] > 0)
        no_right = (i == blocks - 1) & (meta[2 * requests + 1] > 0)
        hidden = ((place < BLK) & no_left) | (
            (place >= 2 * BLK) & (place < 3 * BLK) & no_right
        )
        s = jnp.where(hidden, -1e30, s)
        e = jnp.exp(s - jnp.max(s, -1, keepdims=True))
        p = e * (1.0 / jnp.sum(e, -1, keepdims=True))
        pb = p.astype(BF16)
        o = merge(jnp.dot(pb, vals, preferred_element_type=F32)).astype(BF16)
        att_ref[here, :] = o
        dp = lax.dot_general(gs, vals, nt, preferred_element_type=F32)
        go = both(g.astype(F32) * o.astype(F32))
        delta = jnp.sum(go, -1, keepdims=True)
        ds = (p * (dp - delta)).astype(BF16)
        dq = merge(jnp.dot(ds, keys, preferred_element_type=F32)) * (DH**-0.5)
        dq_ref[here, :] = dq.astype(BF16)
        dkl = lax.dot_general(ds, qs, tn, preferred_element_type=F32)
        dvl = lax.dot_general(pb, gs, tn, preferred_element_type=F32)
        dk_ref[window, :] += dkl[: 3 * BLK]
        dv_ref[window, :] += dvl[: 3 * BLK]
        for r, (owner, at_k, at_v) in enumerate(spots):
            at = (3 + r) * BLK
            back[owner, at_k, :] = dkl[at : at + BLK].astype(BF16)
            back[owner, at_v, :] = dvl[at : at + BLK].astype(BF16)
        dks[...] += dkl[near:]
        dvs[...] += dvl[near:]
        return carry

    lax.fori_loop(0, blocks, step, 0)
    back[:, sum_at : sum_at + SUMR, :] = dks[...].astype(BF16).reshape(shards, SUMR, LANES)
    back[:, sum_at + SUMR : weight_at, :] = dvs[...].astype(BF16).reshape(shards, SUMR, LANES)
    terms = jnp.dot(gft_ref[...], att_ref[...], preferred_element_type=F32)
    back[:, weight_at:, :] = terms.astype(BF16).reshape(shards, weight_rows, LANES)


def combine_kernel(
    capacity, asked, dk_ref, dv_ref, prev_ref, next_ref, back, gk_ref, gv_ref, gw_ref, acc
):
    shards = back.shape[0]
    tokens = gk_ref.shape[0]
    sum_at = 2 * capacity * BLK
    weight_at = sum_at + 2 * SUMR
    for j, (own, out) in enumerate(((dk_ref, gk_ref), (dv_ref, gv_ref))):
        acc[...] = own[BLK : BLK + tokens, :]
        half = slice(j * BLK, (j + 1) * BLK)
        acc[:BLK, :] += prev_ref[half, :].astype(F32)
        acc[tokens - BLK :, :] += next_ref[half, :].astype(F32)
        at = sum_at + j * SUMR
        acc[:SUMR, :] += jnp.sum(back[:, at : at + SUMR, :].astype(F32), 0)

        def add(slot, carry):
            block = asked[slot]

            @pl.when(block >= 0)
            def _():
                rows = pl.ds(pl.multiple_of(block * BLK, BLK), BLK)
                rank = j * capacity + lax.rem(slot, capacity)
                spot = pl.ds(pl.multiple_of(rank * BLK, BLK), BLK)
                acc[rows, :] += back[lax.div(slot, capacity), spot, :].astype(F32)

            return carry

        lax.fori_loop(0, shards * capacity, add, 0)
        out[...] = acc[...].astype(BF16)
    gw_ref[...] = jnp.sum(back[:, weight_at:, :].astype(F32), 0)


def per_device(queries, keys, values, partners, out_weight, grad_out):
    shards = lax.axis_size("seq")
    my_shard = lax.axis_index("seq")
    my_half = lax.axis_index("head")
    tokens, width = queries.shape
    model = out_weight.shape[1]
    blocks = tokens // BLK
    capacity = (R * blocks + shards - 1) // shards
    requests = blocks * R
    chunks = CHUNKS
    cwidth = width // chunks
    pairs = cwidth // LANES
    sent_rows = 2 * capacity * BLK + 2 * SUMR
    back_rows = sent_rows + model // shards
    nsum = shards * SUMR
    total = (3 + R) * BLK + nsum
    up = [(i, i + 1) for i in range(shards - 1)]
    down = [(i + 1, i) for i in range(shards - 1)]
    swap = [(0, 1), (1, 0)]
    params = pltpu.CompilerParams(vmem_limit_bytes=VMEM)

    wanted = partners.reshape(-1)
    owners = wanted // blocks
    inside = wanted % blocks
    order = jnp.arange(requests)
    earlier = (owners[:, None] == owners[None, :]) & (order[None, :] < order[:, None])
    ranks = jnp.sum(earlier.astype(jnp.int32), 1)
    slots = owners * capacity + ranks
    hits = (slots[:, None] == jnp.arange(shards * capacity)[None, :]).astype(jnp.int32)
    asks = (jnp.sum(hits * (inside[:, None] + 1), 0) - 1).reshape(shards, capacity)
    asked = lax.all_to_all(asks, "seq", split_axis=0, concat_axis=0, tiled=True).reshape(-1)
    ends = jnp.stack([my_shard == 0, my_shard == shards - 1]).astype(jnp.int32)
    meta = jnp.concatenate([owners, ranks, ends])

    whole = pl.BlockSpec((tokens, width), lambda s, m: (0, 0))
    sent = pl.pallas_call(
        functools.partial(pack_kernel, capacity, chunks),
        out_shape=[jax.ShapeDtypeStruct((shards, sent_rows, cwidth), BF16)] * chunks,
        grid_spec=pltpu.PrefetchScalarGridSpec(
            num_scalar_prefetch=1,
            grid=(shards,),
            in_specs=[whole, whole],
            out_specs=[pl.BlockSpec((1, sent_rows, cwidth), lambda s, m: (s, 0, 0))] * chunks,
        ),
        compiler_params=params,
        name="pack",
    )(asked, keys, values)
    arrived = [
        lax.all_to_all(x, "seq", split_axis=0, concat_axis=0, tiled=True) for x in sent
    ]

    tail = jnp.concatenate([keys[tokens - BLK :], values[tokens - BLK :]], 0)
    lead = jnp.concatenate([keys[:BLK], values[:BLK]], 0)
    before = lax.ppermute(tail, "seq", up)
    after = lax.ppermute(lead, "seq", down)
    k_pad = jnp.concatenate([before[:BLK], keys, after[:BLK]], 0)
    v_pad = jnp.concatenate([before[BLK:], values, after[BLK:]], 0)
    grad_full = lax.all_gather(grad_out, "head", axis=0, tiled=True)
    weight_other = lax.ppermute(out_weight, "head", swap)
    grad_attended = lax.dot_general(
        grad_full, out_weight, (((1,), (1,)), ((), ())), preferred_element_type=F32
    ).astype(BF16)
    grad_turned = grad_full.T

    results = []
    for c in range(chunks):
        column = lambda p, m, c=c: (0, c * pairs + p)
        local = lambda p, m: (0, p)
        local3 = lambda p, m: (0, 0, p)
        results.append(
            pl.pallas_call(
                functools.partial(attend_kernel, capacity),
                out_shape=[
                    jax.ShapeDtypeStruct((tokens, cwidth), BF16),
                    jax.ShapeDtypeStruct((tokens, cwidth), BF16),
                    jax.ShapeDtypeStruct((tokens + 2 * BLK, cwidth), F32),
                    jax.ShapeDtypeStruct((tokens + 2 * BLK, cwidth), F32),
                    jax.ShapeDtypeStruct((shards, back_rows, cwidth), BF16),
                ],
                grid_spec=pltpu.PrefetchScalarGridSpec(
                    num_scalar_prefetch=1,
                    grid=(pairs,),
                    in_specs=[
                        pl.BlockSpec((tokens, LANES), column),
                        pl.BlockSpec((tokens + 2 * BLK, LANES), column),
                        pl.BlockSpec((tokens + 2 * BLK, LANES), column),
                        pl.BlockSpec((shards, sent_rows, LANES), local3),
                        pl.BlockSpec((tokens, LANES), column),
                        pl.BlockSpec((model, tokens), lambda p, m: (0, 0)),
                    ],
                    out_specs=[
                        pl.BlockSpec((tokens, LANES), local),
                        pl.BlockSpec((tokens, LANES), local),
                        pl.BlockSpec((tokens + 2 * BLK, LANES), local),
                        pl.BlockSpec((tokens + 2 * BLK, LANES), local),
                        pl.BlockSpec((shards, back_rows, LANES), local3),
                    ],
                    scratch_shapes=[
                        pltpu.VMEM((total, LANES), BF16),
                        pltpu.VMEM((total, LANES), BF16),
                        pltpu.VMEM((nsum, LANES), F32),
                        pltpu.VMEM((nsum, LANES), F32),
                    ],
                ),
                compiler_params=params,
                cost_estimate=pl.CostEstimate(
                    flops=12 * tokens * total * LANES * pairs * 4,
                    bytes_accessed=8 * tokens * cwidth * 2,
                    transcendentals=tokens * total * 2 * pairs,
                ),
                name="attend",
            )(meta, queries, k_pad, v_pad, arrived[c], grad_attended, grad_turned)
        )

    finals = []
    for c in range(chunks):
        dk, dv, back = results[c][2:]
        returned = lax.all_to_all(back, "seq", split_axis=0, concat_axis=0, tiled=True)
        to_prev = jnp.concatenate([dk[:BLK], dv[:BLK]], 0).astype(BF16)
        to_next = jnp.concatenate([dk[tokens + BLK :], dv[tokens + BLK :]], 0).astype(BF16)
        from_next = lax.ppermute(to_prev, "seq", down)
        from_prev = lax.ppermute(to_next, "seq", up)
        local = lambda p, m: (0, p)
        finals.append(
            pl.pallas_call(
                functools.partial(combine_kernel, capacity),
                out_shape=[
                    jax.ShapeDtypeStruct((tokens, cwidth), BF16),
                    jax.ShapeDtypeStruct((tokens, cwidth), BF16),
                    jax.ShapeDtypeStruct((model // shards, cwidth), F32),
                ],
                grid_spec=pltpu.PrefetchScalarGridSpec(
                    num_scalar_prefetch=1,
                    grid=(pairs,),
                    in_specs=[
                        pl.BlockSpec((tokens + 2 * BLK, LANES), local),
                        pl.BlockSpec((tokens + 2 * BLK, LANES), local),
                        pl.BlockSpec((2 * BLK, LANES), local),
                        pl.BlockSpec((2 * BLK, LANES), local),
                        pl.BlockSpec((shards, back_rows, LANES), lambda p, m: (0, 0, p)),
                    ],
                    out_specs=[
                        pl.BlockSpec((tokens, LANES), local),
                        pl.BlockSpec((tokens, LANES), local),
                        pl.BlockSpec((model // shards, LANES), local),
                    ],
                    scratch_shapes=[pltpu.VMEM((tokens, LANES), F32)],
                ),
                compiler_params=params,
                name="combine",
            )(asked, dk, dv, from_prev, from_next, returned)
        )

    def join(parts):
        return parts[0] if chunks == 1 else jnp.concatenate(parts, 1)

    attended = join([r[0] for r in results])
    half = tokens // 2
    mine = lax.dynamic_slice_in_dim(attended, my_half * half, half, 0)
    others = lax.dynamic_slice_in_dim(attended, (1 - my_half) * half, half, 0)
    received = lax.ppermute(others, "head", swap)
    mixed = jnp.dot(mine, out_weight, preferred_element_type=F32) + jnp.dot(
        received, weight_other, preferred_element_type=F32
    )
    return (
        mixed.astype(BF16),
        join([r[1] for r in results]),
        join([f[0] for f in finals]),
        join([f[1] for f in finals]),
        join([f[2] for f in finals]).T,
    )


def solution(mesh):
    in_specs = (
        P("seq", "head"),
        P("seq", "head"),
        P("seq", "head"),
        P("seq", None),
        P("head", None),
        P(("seq", "head"), None),
    )
    out_specs = (
        P(("seq", "head"), None),
        P("seq", "head"),
        P("seq", "head"),
        P("seq", "head"),
        P("head", "seq"),
    )
    return jax.shard_map(
        per_device, mesh=mesh, in_specs=in_specs, out_specs=out_specs, check_vma=False
    )
```

time: 834 us -> 468 us (0.56); the launches traced: 823 us -> 467 us
  local copies, waits for them, and re-layouts: 214 us -> 14 us
  matrix products: 168 us -> 7.86 us
  blocking collectives: 143 us -> 10.2 us
  waiting for transfers between devices: 169 us -> 301 us
  Pallas kernels: 0 us -> 91.1 us
  other arithmetic: 80.7 us -> 2.67 us
    ppermute x4 -> x6, waiting for transfers between devices: 110 us -> 301 us  [the longest x1 141 us: per_device(): before = lax.ppermute(tail, 'seq', up)]
    dot_general x115 -> x2, matrix products: 164 us -> 3.64 us  [the longest x1 2.91 us: per_device(): jnp.dot(received, weight_other, preferred_element_type=F32)]
    all_gather x1 -> x0, blocking collectives: 143 us -> none  [per_device(): lax.all_gather(own_blocks[:, 0, :SUMR], 'seq', axis=1, tiled=True)]
    pallas_call x0 -> x3, Pallas kernels: none -> 91.1 us  [the longest x1 70.2 us: per_device(): pl.pallas_call(functools.partial(attend_kernel, capacity), out_shape=[jax...]
    reduce_scatter x3 -> x0, waiting for transfers between devices: 57.4 us -> none  [the longest x1 35.5 us: per_device(): lax.psum_scatter(jnp.dot(attended, out_weight, preferred_element_type=jnp...]
    another operation x12 -> x0, local copies, waits for them, and re-layouts: 47.6 us -> none  [the longest x2 25.5 us: per_device(): jnp.stack([from_heads(results[1]), from_heads(results[2])], 0)]
    slice x13 -> x5, local copies, waits for them, and re-layouts: 38 us -> 0.06 us  [the longest x2 0.02 us: per_device(): to_prev = jnp.concatenate([dk[:BLK], dv[:BLK]], 0).astype(BF16)]
    concatenate x6 -> x0, local copies, waits for them, and re-layouts: 34.6 us -> none  [the longest x2 17.3 us: per_device(): value_sequence = jnp.concatenate([window[1], chosen[1]], 1)]
  transfers between devices with their start and end apart: 11 -> 9, of which waited for: 4 -> 5; matrix products, arithmetic and copies ran while one was open for 11% -> 2% of each run, Pallas kernels for 0% -> 0%
where the time goes in v1:
time: 468 us; the launch traced here: 467 us
  waiting for transfers between devices  301 us (64%)
  Pallas kernels  91.1 us (19%)
  starting transfers between devices  25.5 us (5%)
  between operations  14.3 us (3%)
  local copies, waits for them, and re-layouts  14 us (3%)
  blocking collectives  10.2 us (2%)
  matrix products  7.86 us (2%)
    ppermute x1, waiting for transfers between devices, per_device(): before = lax.ppermute(tail, 'seq', up)  141 us
    ppermute x1, waiting for transfers between devices, per_device(): from_next = lax.ppermute(to_prev, 'seq', down)  133 us
    pallas_call x1, Pallas kernels, per_device(): pl.pallas_call(functools.partial(attend_kernel, capacity), out_shape=[jax...  70.2 us
    ppermute x1, waiting for transfers between devices, per_device(): weight_other = lax.ppermute(out_weight, 'head', swap)  14.3 us
    pallas_call x1, Pallas kernels, per_device(): pl.pallas_call(functools.partial(combine_kernel, capacity), out_shape=[ja...  13.8 us
    unnamed x34, local copies, waits for them, and re-layouts  13.1 us
    ppermute x1, waiting for transfers between devices, per_device(): received = lax.ppermute(others, 'head', swap)  11.2 us
    all_to_all x1, blocking collectives, per_device(): lax.all_to_all(asks, 'seq', split_axis=0, concat_axis=0, tiled=True)  10.2 us
  transfers between devices with their start and end apart: 9, of which 5 were waited for; matrix products, arithmetic and copies ran while one was open for 2% of the time, Pallas kernels for 0%

profile of v1, /device:TPU:11, one launch (start us, length us, event | category | flops | bytes accessed | tf_op | source)
XLA Modules:
  0.0 466.8 jit_solution(1447682256123291624)
XLA Ops:
  7.2 0.8 copy.18
  7.9 0.1 reshape.125
  8.0 0.2 convert_reduce_fusion
  8.2 0.1 select_reduce_fusion
  8.3 0.1 sub.17
  8.4 10.2 %all_to_all.16 = s32[16,1,3]{2,1,0:T(1,128)S(1)} all-to-all(s32[16,1,3]{2,1,0:T(1,128)S(1)} %bitcast.10), channel_id=1, replica_groups=mesh['seq'=16,'head'=2] {'seq'}, dimensions={0} | all-to-all | bytes 384 | tf_op jit(solution)/shard_map/all_to_all | solution.py:189
  18.6 0.5 broadcast.145
  19.1 0.7 reduce.3
  19.8 0.1 reshape.126.asked
  19.9 1.2 copy-done.3
  21.1 1.2 copy-done.5
  22.3 7.1 %pack.1 = bf16[16,416,512]{2,1,0:T(8,128)(2,1)} custom-call(s32[48]{0:T(128)S(1)} %reshape.126.asked, bf16[1024,512]{1,0:T(8,128)(2,1)S(1)} %copy-done.5, bf16[1024,512]{1,0:T(8,128)(2,1)S(1)} %copy-done.3), custom_call_target="tpu_custom_call" | custom-call | tf_op jit(solution)/shard_map/pack/pallas_call | solution.py:194
  29.4 7.3 %all-to-all-start.1 = ((bf16[16,416,512]{2,1,0:T(8,128)(2,1)}), bf16[16,416,512]{2,1,0:T(8,128)(2,1)}, u32[]{:S(2)}, u32[]{:S(2)}) async-start(bf16[16,416,512]{2,1,0:T(8,128)(2,1)} %pack.1), calls=%async_computation.1 | async-start | bytes 13631488 | tf_op jit(solution)/shard_map/all_to_all | solution.py:207
  36.7 0.0 copy-start.6
  36.7 0.0 all-gather.2.cloned.1.call-start
  36.8 1.3 copy.20
  38.1 0.0 all-gather.2.cloned.1.call-update
  38.1 0.5 copy-done.6
  38.7 3.4 collective-permute-start
  42.0 1.9 collective-permute-start.1
  44.0 0.1 add_convert_fusion.1
  44.1 0.1 pad_add_fusion.meta
  44.1 140.8 %collective-permute-done = bf16[128,512]{1,0:T(8,128)(2,1)S(1)} collective-permute-done((bf16[128,512]{1,0:T(8,128)(2,1)S(1)}, bf16[128,512]{1,0:T(8,128)(2,1)S(1)}, u32[]{:S(2)}, u32[]{:S(2)}) %collective-permute-start) | collective-permute-done | bytes 131104 | tf_op jit(solution)/shard_map/ppermute | solution.py:212
  184.9 1.7 collective-permute-done.1
  186.7 0.1 pad_maximum_fusion.1.v_ref
  186.8 1.1 pad_maximum_fusion.k_ref
  187.9 4.2 convolution_convert_fusion.g_ref
  192.1 1.2 copy-done.12
  193.3 1.2 copy-done.13
  194.6 70.2 %attend.1 = (bf16[1024,512]{1,0:T(8,128)(2,1)S(1)}, bf16[1024,512]{1,0:T(8,128)(2,1)}, f32[1152,512]{1,0:T(8,128)}, f32[1152,512]{1,0:T(8,128)}, bf16[16,480,512]{2,1,0:T(8,128)(2,1)}) custom-call(s32[98]{0:T(128)S(1)} %pad_add_fusion.meta, bf16[1024,512]{1,0:T(8,128)(2,1)S(1)} %copy-done.12, bf16[1152,512]{1,0:T(8,128)(2,1)S(1)} %copy-done.7, ...), custom_call_target="tpu_custom_call" | custom-call | flops 16106127360 | bytes 8388608 | tf_op jit(solution)/shard_map/attend/pallas_call | solution.py:229
  264.7 1.0 copy-done.8
  265.7 4.9 %all-to-all-start.2 = ((bf16[16,480,512]{2,1,0:T(8,128)(2,1)}), bf16[16,480,512]{2,1,0:T(8,128)(2,1)}, u32[]{:S(2)}, u32[]{:S(2)}) async-start(bf16[16,480,512]{2,1,0:T(8,128)(2,1)} %get-tuple-element.17), calls=%async_computation.2 | async-start | bytes 15728640 | tf_op jit(solution)/shard_map/all_to_all | solution.py:276
  270.6 1.3 collective-permute-start.3
  272.0 0.2 convert.12
  272.1 1.5 copy-done.1
  273.6 0.2 convert.13
  273.7 0.3 collective-permute-start.2
  274.1 2.6 collective-permute-start.5
  276.7 3.8 collective-permute-start.4
  280.6 0.7 fusion
  281.3 14.3 %collective-permute-done.3 = bf16[512,1024]{1,0:T(8,128)(2,1)} collective-permute-done((bf16[512,1024]{1,0:T(8,128)(2,1)}, bf16[512,1024]{1,0:T(8,128)(2,1)}, u32[]{:S(2)}, u32[]{:S(2)}) %collective-permute-start.3) | collective-permute-done | bytes 1048608 | tf_op jit(solution)/shard_map/ppermute | solution.py:217
  295.6 11.2 %collective-permute-done.2 = bf16[512,512]{1,0:T(8,128)(2,1)S(1)} collective-permute-done((bf16[512,512]{1,0:T(8,128)(2,1)S(1)}, bf16[512,512]{1,0:T(8,128)(2,1)S(1)}, u32[]{:S(2)}, u32[]{:S(2)}) %collective-permute-start.2) | collective-permute-done | bytes 524320 | tf_op jit(solution)/shard_map/ppermute | solution.py:319
  306.8 2.9 add_convert_fusion
  309.7 133.1 %collective-permute-done.5.next_ref = bf16[128,512]{1,0:T(8,128)(2,1)S(1)} collective-permute-done((bf16[128,512]{1,0:T(8,128)(2,1)S(1)}, bf16[128,512]{1,0:T(8,128)(2,1)S(1)}, u32[]{:S(2)}, u32[]{:S(2)}) %collective-permute-start.5) | collective-permute-done | bytes 131104 | tf_op jit(solution)/shard_map/ppermute | solution.py:279
  442.9 0.7 copy-done.10
  443.5 1.7 copy-done.2
  445.2 0.9 copy-done.11
  446.1 13.8 %combine.1 = (bf16[1024,512]{1,0:T(8,128)(2,1)}, bf16[1024,512]{1,0:T(8,128)(2,1)}, f32[64,512]{1,0:T(8,128)}) custom-call(s32[48]{0:T(128)S(1)} %reshape.126.asked, f32[1152,512]{1,0:T(8,128)S(1)} %copy-done, f32[1152,512]{1,0:T(8,128)S(1)} %copy-done.2, bf16[128,512]{1,0:T(8,128)(2,1)S(1)} %copy-done.11, ...), custom_call_target="tpu_custom_call" | custom-call | tf_op jit(solution)/shard_map/combine/pallas_call | solution.py:283
  (38 shorter events, 0.2 us)
Async XLA Ops:
  19.8 1.2 copy-start.3
  21.1 1.2 copy-start.5
  29.4 7.4 %copy-start.14 = (bf16[512,1024]{1,0:T(8,128)(2,1)S(1)}, bf16[512,1024]{1,0:T(8,128)(2,1)}, u32[]{:S(2)}) copy-start(bf16[512,1024]{1,0:T(8,128)(2,1)} %param.11) | copy-start | bytes 3145732
  29.4 162.7 %all-to-all-start.1 = ((bf16[16,416,512]{2,1,0:T(8,128)(2,1)}), bf16[16,416,512]{2,1,0:T(8,128)(2,1)}, u32[]{:S(2)}, u32[]{:S(2)}) async-start(bf16[16,416,512]{2,1,0:T(8,128)(2,1)} %pack.1), calls=%async_computation.1 | async-start | bytes 13631488 | tf_op jit(solution)/shard_map/all_to_all | solution.py:207
  36.7 1.4 copy-start.4
  36.7 1.9 copy-start.6
  36.7 151.2 %all-gather.2.cloned.1.call-start = ((), (), s32[]{:S(2)}) async-start(), calls=%async_computation.3 | async-start | bytes 3145728 | tf_op jit(solution)/shard_map/all_gather | solution.py:216
  38.7 146.3 %collective-permute-start = (bf16[128,512]{1,0:T(8,128)(2,1)S(1)}, bf16[128,512]{1,0:T(8,128)(2,1)S(1)}, u32[]{:S(2)}, u32[]{:S(2)}) collective-permute-start(bf16[128,512]{1,0:T(8,128)(2,1)S(1)} %pad_maximum_fusion.2), channel_id=1, source_target_pairs={{0,2},{2,4},{4,6},{6,8},{8,10},{10,12},{12,14},{14,16},{16,18},{18... | collective-permute-start | bytes 393224 | tf_op jit(solution)/shard_map/ppermute | solution.py:212
  42.0 144.6 %collective-permute-start.1 = (bf16[128,512]{1,0:T(8,128)(2,1)S(1)}, bf16[128,512]{1,0:T(8,128)(2,1)S(1)}, u32[]{:S(2)}, u32[]{:S(2)}) collective-permute-start(bf16[128,512]{1,0:T(8,128)(2,1)S(1)} %pad_maximum_fusion.3), channel_id=1, source_target_pairs={{2,0},{4,2},{6,4},{8,6},{10,8},{12,10},{14,12},{16,14},{18,16},{20... | collective-permute-start | bytes 393224 | tf_op jit(solution)/shard_map/ppermute | solution.py:213
  187.9 4.2 copy-start.7
  192.1 1.2 copy-start.12
  193.3 1.2 copy-start.13
  264.7 1.0 copy-start.8
  265.7 6.2 %copy-start.9 = (bf16[1024,512]{1,0:T(8,128)(2,1)S(1)}, bf16[1024,512]{1,0:T(8,128)(2,1)}, u32[]{:S(2)}) copy-start(bf16[1024,512]{1,0:T(8,128)(2,1)} %copy-done.8) | copy-start | bytes 3145732
  265.7 6.2 %copy-start = (f32[1152,512]{1,0:T(8,128)S(1)}, f32[1152,512]{1,0:T(8,128)}, u32[]{:S(2)}) copy-start(f32[1152,512]{1,0:T(8,128)} %get-tuple-element.15.dk_ref) | copy-start | bytes 7077892
  265.7 177.8 %all-to-all-start.2 = ((bf16[16,480,512]{2,1,0:T(8,128)(2,1)}), bf16[16,480,512]{2,1,0:T(8,128)(2,1)}, u32[]{:S(2)}, u32[]{:S(2)}) async-start(bf16[16,480,512]{2,1,0:T(8,128)(2,1)} %get-tuple-element.17), calls=%async_computation.2 | async-start | bytes 15728640 | tf_op jit(solution)/shard_map/all_to_all | solution.py:276
  270.6 25.0 %collective-permute-start.3 = (bf16[512,1024]{1,0:T(8,128)(2,1)}, bf16[512,1024]{1,0:T(8,128)(2,1)}, u32[]{:S(2)}, u32[]{:S(2)}) collective-permute-start(bf16[512,1024]{1,0:T(8,128)(2,1)} %param.10), channel_id=1, source_target_pairs={{0,1},{1,0},{2,3},{3,2},{4,5},{5,4},{6,7},{7,6},{8,9},{9,8},{10,11... | collective-permute-start | bytes 3145736 | tf_op jit(solution)/shard_map/ppermute | solution.py:217
  271.9 1.7 copy-start.1
  273.6 7.0 %copy-start.15 = (bf16[512,1024]{1,0:T(8,128)(2,1)S(1)}, bf16[512,1024]{1,0:T(8,128)(2,1)}, u32[]{:S(2)}) copy-start(bf16[512,1024]{1,0:T(8,128)(2,1)} %param.10) | copy-start | bytes 3145732
  273.7 33.1 %collective-permute-start.2 = (bf16[512,512]{1,0:T(8,128)(2,1)S(1)}, bf16[512,512]{1,0:T(8,128)(2,1)S(1)}, u32[]{:S(2)}, u32[]{:S(2)}) collective-permute-start(bf16[512,512]{1,0:T(8,128)(2,1)S(1)} %constant_dynamic-slice_fusion), channel_id=1, source_target_pairs={{0,1},{1,0},{2,3},{3,2},{4,5},{5,4},{6,7},{7,6},{8,9},{9,8},{10,11... | collective-permute-start | bytes 1572872 | tf_op jit(solution)/shard_map/ppermute | solution.py:319
  274.1 168.8 %collective-permute-start.5 = (bf16[128,512]{1,0:T(8,128)(2,1)S(1)}, bf16[128,512]{1,0:T(8,128)(2,1)S(1)}, u32[]{:S(2)}, u32[]{:S(2)}) collective-permute-start(bf16[128,512]{1,0:T(8,128)(2,1)S(1)} %pad_maximum_fusion.5), channel_id=1, source_target_pairs={{2,0},{4,2},{6,4},{8,6},{10,8},{12,10},{14,12},{16,14},{18,16},{20... | collective-permute-start | bytes 393224 | tf_op jit(solution)/shard_map/ppermute | solution.py:279
  276.7 166.1 %collective-permute-start.4 = (bf16[128,512]{1,0:T(8,128)(2,1)S(1)}, bf16[128,512]{1,0:T(8,128)(2,1)S(1)}, u32[]{:S(2)}, u32[]{:S(2)}) collective-permute-start(bf16[128,512]{1,0:T(8,128)(2,1)S(1)} %pad_maximum_fusion.4), channel_id=1, source_target_pairs={{0,2},{2,4},{4,6},{6,8},{8,10},{10,12},{12,14},{14,16},{16,18},{18... | collective-permute-start | bytes 393224 | tf_op jit(solution)/shard_map/ppermute | solution.py:280
  442.9 0.7 copy-start.10
  443.5 1.7 copy-start.2
  445.2 0.9 copy-start.11
Sparse Core Ops, SparseCore 0:
  39.7 33.7 all-gather.1

commit v2 on v1

v2 whole, which is shorter than its diff:
```python
import functools

import jax
import jax.numpy as jnp
from jax import lax
from jax.experimental import pallas as pl
from jax.experimental.pallas import tpu as pltpu
from jax.sharding import PartitionSpec as P

DH = 64
BLK = 64
R = 3
SUMR = 16
LANES = 128
VMEM = 58 * 1024 * 1024
F32 = jnp.float32
BF16 = jnp.bfloat16

MESH = pl.DeviceIdType.MESH


def pack_kernel(capacity, asked, k_ref, v_ref, out):
    shard = pl.program_id(0)
    for c in range(out.shape[0]):
        cols = slice(c * LANES, (c + 1) * LANES)
        for j, src in enumerate((k_ref, v_ref)):
            for n in range(capacity):
                block = jnp.maximum(asked[shard * capacity + n], 0)
                rows = pl.ds(pl.multiple_of(block * BLK, BLK), BLK)
                at = (j * capacity + n) * BLK
                out[c, 0, at : at + BLK, :] = src[rows, cols]
            at = 2 * capacity * BLK + j * SUMR
            out[c, 0, at : at + SUMR, :] = src[0:SUMR, cols]


def attend_kernel(
    shards, capacity,
    meta, q_ref, w_ref, wo_ref, k_hbm, v_hbm, go_hbm, sent,
    mixed_ref, dq_ref, dk_ref, dv_ref, returned, halo_in,
    kpad, vpad, gf, g_all, att, received, arrived, cur_k, cur_v, part_k, part_v, back, halo_out,
    kl, vl, dka, dva, dks, dvs,
    local_sem, halo_send, halo_recv, go_send, go_recv, out_send, out_recv,
    ret_send, ret_recv, edge_send, edge_recv, att_send, att_recv,
):
    tokens, width = q_ref.shape
    model = w_ref.shape[1]
    half = tokens // 2
    blocks = tokens // BLK
    pairs = width // LANES
    requests = blocks * R
    nsum = shards * SUMR
    near = (3 + R) * BLK
    total = near + nsum
    sum_at = 2 * capacity * BLK
    weight_at = sum_at + 2 * SUMR
    weight_rows = model // shards
    me = lax.axis_index("seq")
    side = lax.axis_index("head")
    after = lax.rem(me + 1, shards)
    before = lax.rem(me + shards - 1, shards)
    other = 1 - side
    first = lax.broadcasted_iota(jnp.int32, (1, LANES), 1) < DH
    place = lax.broadcasted_iota(jnp.int32, (1, total), 1)
    nt = (((1,), (1,)), ((), ()))
    tn = (((0,), (0,)), ((), ()))

    barrier = pltpu.get_barrier_semaphore()

    def greet(k, carry):
        pl.semaphore_signal(
            barrier, inc=1, device_id={"seq": lax.rem(me + k, shards)}, device_id_type=MESH
        )
        return carry

    lax.fori_loop(1, shards, greet, 0)
    pl.semaphore_signal(barrier, inc=1, device_id={"head": other}, device_id_type=MESH)
    pl.semaphore_wait(barrier, shards)

    def remote(src, dst, send, recv, to):
        return pltpu.make_async_remote_copy(
            src_ref=src, dst_ref=dst, send_sem=send, recv_sem=recv,
            device_id=to, device_id_type=MESH,
        )

    middle = pl.ds(BLK, tokens)
    near_copies = [
        remote(k_hbm.at[pl.ds(tokens - BLK, BLK)], kpad.at[pl.ds(0, BLK)],
               halo_send.at[0], halo_recv.at[0], {"seq": after}),
        remote(k_hbm.at[pl.ds(0, BLK)], kpad.at[pl.ds(BLK + tokens, BLK)],
               halo_send.at[1], halo_recv.at[1], {"seq": before}),
        remote(v_hbm.at[pl.ds(tokens - BLK, BLK)], vpad.at[pl.ds(0, BLK)],
               halo_send.at[2], halo_recv.at[2], {"seq": after}),
        remote(v_hbm.at[pl.ds(0, BLK)], vpad.at[pl.ds(BLK + tokens, BLK)],
               halo_send.at[3], halo_recv.at[3], {"seq": before}),
    ]
    my_rows = pl.ds(pl.multiple_of(side * half, half), half)
    other_rows = pl.ds(pl.multiple_of(other * half, half), half)
    go_copy = remote(go_hbm, gf.at[my_rows], go_send, go_recv, {"head": other})
    own_copies = [
        pltpu.make_async_copy(k_hbm, kpad.at[middle], local_sem.at[0]),
        pltpu.make_async_copy(v_hbm, vpad.at[middle], local_sem.at[1]),
        pltpu.make_async_copy(go_hbm, gf.at[my_rows], local_sem.at[2]),
    ]
    for copy in near_copies + [go_copy] + own_copies:
        copy.start()

    def send_pair(c, carry):
        def send(k, carry):
            to = lax.rem(me + k, shards)
            remote(sent.at[c, to], arrived.at[c, me], out_send.at[c, k], out_recv.at[c, k],
                   {"seq": to}).start()
            return carry

        lax.fori_loop(1, shards, send, 0)
        pltpu.make_async_copy(sent.at[c, me], arrived.at[c, me], out_recv.at[c, 0]).start()
        return carry

    lax.fori_loop(0, pairs, send_pair, 0)

    for copy in own_copies + [go_copy]:
        copy.wait()

    def project(j, carry):
        rows = pl.ds(pl.multiple_of(j * 256, 256), 256)
        g_all[rows, :] = lax.dot_general(
            gf[rows, :], w_ref[...], nt, preferred_element_type=F32
        ).astype(BF16)
        return carry

    lax.fori_loop(0, tokens // 256, project, 0)
    for copy in near_copies:
        copy.wait()

    def both(x):
        zero = jnp.zeros_like(x)
        return jnp.concatenate([jnp.where(first, x, zero), jnp.where(first, zero, x)], 0)

    def merge(x):
        return jnp.where(first, x[:BLK], x[BLK:])

    def edge_copies(c):
        return [
            remote(halo_out.at[c, 1], halo_in.at[c, 0], edge_send.at[c, 0], edge_recv.at[c, 0],
                   {"seq": after}),
            remote(halo_out.at[c, 0], halo_in.at[c, 1], edge_send.at[c, 1], edge_recv.at[c, 1],
                   {"seq": before}),
        ]

    def att_copy(c):
        return remote(att.at[c, other_rows], received.at[c], att_send.at[c], att_recv.at[c],
                      {"head": other})

    def pair(c, carry):
        cols = pl.ds(pl.multiple_of(c * LANES, LANES), LANES)

        def landed(k, carry):
            source = lax.rem(me + shards - k, shards)
            remote(sent.at[c, source], arrived.at[c, source], out_send.at[c, k],
                   out_recv.at[c, k], {"seq": source}).wait_recv()
            return carry

        lax.fori_loop(1, shards, landed, 0)
        pltpu.make_async_copy(sent.at[c, me], arrived.at[c, me], out_recv.at[c, 0]).wait()

        def take(d, carry):
            for n in range(capacity):
                at = n * BLK
                cur_k[d * capacity + n] = arrived[c, d, at : at + BLK, :]
                at = (capacity + n) * BLK
                cur_v[d * capacity + n] = arrived[c, d, at : at + BLK, :]
            return carry

        lax.fori_loop(0, shards, take, 0)
        kl[near:, :] = arrived[c, :, sum_at : sum_at + SUMR, :].reshape(nsum, LANES)
        vl[near:, :] = arrived[c, :, sum_at + SUMR : weight_at, :].reshape(nsum, LANES)
        for ref in (dka, dva, dks, dvs):
            ref[...] = jnp.zeros_like(ref)

        def step(i, carry):
            row = pl.multiple_of(i * BLK, BLK)
            here = pl.ds(row, BLK)
            window = pl.ds(row, 3 * BLK)
            kl[0 : 3 * BLK, :] = kpad[window, cols]
            vl[0 : 3 * BLK, :] = vpad[window, cols]
            for r in range(R):
                slot = meta[i * R + r]
                at = (3 + r) * BLK
                kl[at : at + BLK, :] = cur_k[slot]
                vl[at : at + BLK, :] = cur_v[slot]
            keys = kl[...]
            vals = vl[...]
            qs = both(q_ref[here, cols] * jnp.asarray(DH**-0.5, BF16))
            g = g_all[here, cols]
            gs = both(g)
            s = lax.dot_general(qs, keys, nt, preferred_element_type=F32)
            no_left = (i == 0) & (me == 0)
            no_right = (i == blocks - 1) & (me == shards - 1)
            hidden = ((place < BLK) & no_left) | (
                (place >= 2 * BLK) & (place < 3 * BLK) & no_right
            )
            s = jnp.where(hidden, -1e30, s)
            e = jnp.exp(s - jnp.max(s, -1, keepdims=True))
            p = e * (1.0 / jnp.sum(e, -1, keepdims=True))
            pb = p.astype(BF16)
            o = merge(jnp.dot(pb, vals, preferred_element_type=F32)).astype(BF16)
            att[c, here, :] = o
            dp = lax.dot_general(gs, vals, nt, preferred_element_type=F32)
            delta = jnp.sum(both(g.astype(F32) * o.astype(F32)), -1, keepdims=True)
            ds = (p * (dp - delta)).astype(BF16)
            dq = merge(jnp.dot(ds, keys, preferred_element_type=F32)) * (DH**-0.5)
            dq_ref[here, cols] = dq.astype(BF16)
            dkl = lax.dot_general(ds, qs, tn, preferred_element_type=F32)
            dvl = lax.dot_general(pb, gs, tn, preferred_element_type=F32)
            dka[window, :] += dkl[: 3 * BLK]
            dva[window, :] += dvl[: 3 * BLK]
            for r in range(R):
                at = (3 + r) * BLK
                part_k[i * R + r] = dkl[at : at + BLK].astype(BF16)
                part_v[i * R + r] = dvl[at : at + BLK].astype(BF16)
            dks[...] += dkl[near:]
            dvs[...] += dvl[near:]
            return carry

        lax.fori_loop(0, blocks, step, 0)
        att_copy(c).start()

        def fill(d, carry):
            for n in range(capacity):
                request = meta[requests + d * capacity + n]
                at = n * BLK
                back[c, d, at : at + BLK, :] = part_k[request]
                at = (capacity + n) * BLK
                back[c, d, at : at + BLK, :] = part_v[request]
            return carry

        lax.fori_loop(0, shards, fill, 0)
        back[c, :, sum_at : sum_at + SUMR, :] = (
            dks[...].astype(BF16).reshape(shards, SUMR, LANES)
        )
        back[c, :, sum_at + SUMR : weight_at, :] = (
            dvs[...].astype(BF16).reshape(shards, SUMR, LANES)
        )
        count = 256 // weight_rows

        def weigh(j, carry):
            columns = pl.ds(pl.multiple_of(j * 256, 256), 256)
            terms = lax.dot_general(gf[:, columns], att[c], tn, preferred_element_type=F32)
            back[c, pl.ds(j * count, count), weight_at:, :] = terms.astype(BF16).reshape(
                count, weight_rows, LANES
            )
            return carry

        lax.fori_loop(0, model // 256, weigh, 0)

        def send(k, carry):
            to = lax.rem(me + k, shards)
            remote(back.at[c, to], returned.at[c, me], ret_send.at[c, k], ret_recv.at[c, k],
                   {"seq": to}).start()
            return carry

        lax.fori_loop(1, shards, send, 0)
        pltpu.make_async_copy(back.at[c, me], returned.at[c, me], ret_recv.at[c, 0]).start()
        dk_ref[:, cols] = dka[BLK : BLK + tokens, :]
        dv_ref[:, cols] = dva[BLK : BLK + tokens, :]
        halo_out[c, 0, :BLK, :] = dka[:BLK, :].astype(BF16)
        halo_out[c, 0, BLK:, :] = dva[:BLK, :].astype(BF16)
        halo_out[c, 1, :BLK, :] = dka[BLK + tokens :, :].astype(BF16)
        halo_out[c, 1, BLK:, :] = dva[BLK + tokens :, :].astype(BF16)
        for copy in edge_copies(c):
            copy.start()
        return carry

    lax.fori_loop(0, pairs, pair, 0)

    def swapped(c, carry):
        att_copy(c).wait()
        return carry

    lax.fori_loop(0, pairs, swapped, 0)

    def mix(j, carry):
        rows = pl.ds(pl.multiple_of(j * LANES, LANES), LANES)
        own = pl.ds(pl.multiple_of(side * half + j * LANES, LANES), LANES)
        mine = jnp.concatenate([att[c, own, :] for c in range(pairs)], 1)
        theirs = jnp.concatenate([received[c, rows, :] for c in range(pairs)], 1)
        mixed = jnp.dot(mine, w_ref[...], preferred_element_type=F32)
        mixed = mixed + jnp.dot(theirs, wo_ref[...], preferred_element_type=F32)
        mixed_ref[rows, :] = mixed.astype(BF16)
        return carry

    lax.fori_loop(0, half // LANES, mix, 0)

    def finish(c, carry):
        def done(k, carry):
            to = lax.rem(me + k, shards)
            source = lax.rem(me + shards - k, shards)
            remote(sent.at[c, to], arrived.at[c, me], out_send.at[c, k], out_recv.at[c, k],
                   {"seq": to}).wait_send()
            remote(back.at[c, to], returned.at[c, me], ret_send.at[c, k], ret_recv.at[c, k],
                   {"seq": to}).wait_send()
            remote(back.at[c, source], returned.at[c, source], ret_send.at[c, k],
                   ret_recv.at[c, k], {"seq": source}).wait_recv()
            return carry

        lax.fori_loop(1, shards, done, 0)
        pltpu.make_async_copy(back.at[c, me], returned.at[c, me], ret_recv.at[c, 0]).wait()
        for copy in edge_copies(c):
            copy.wait()
        return carry

    lax.fori_loop(0, pairs, finish, 0)


def combine_kernel(capacity, asked, dk_ref, dv_ref, halo, back, gk_ref, gv_ref, gw_ref, acc):
    shards = back.shape[1]
    tokens = gk_ref.shape[0]
    sum_at = 2 * capacity * BLK
    weight_at = sum_at + 2 * SUMR
    for j, (own, out) in enumerate(((dk_ref, gk_ref), (dv_ref, gv_ref))):
        acc[...] = own[...]
        side = slice(j * BLK, (j + 1) * BLK)
        acc[:BLK, :] += halo[0, 0, side, :].astype(F32)
        acc[tokens - BLK :, :] += halo[0, 1, side, :].astype(F32)
        at = sum_at + j * SUMR
        acc[:SUMR, :] += jnp.sum(back[0, :, at : at + SUMR, :].astype(F32), 0)

        def add(shard, carry):
            for n in range(capacity):
                block = asked[shard * capacity + n]
                spot = slice((j * capacity + n) * BLK, (j * capacity + n + 1) * BLK)

                @pl.when(block >= 0)
                def _():
                    rows = pl.ds(pl.multiple_of(block * BLK, BLK), BLK)
                    acc[rows, :] += back[0, shard, spot, :].astype(F32)

            return carry

        lax.fori_loop(0, shards, add, 0)
        out[...] = acc[...].astype(BF16)
    gw_ref[...] = jnp.sum(back[0, :, weight_at:, :].astype(F32), 0)


def per_device(queries, keys, values, partners, out_weight, grad_out):
    shards = lax.axis_size("seq")
    tokens, width = queries.shape
    model = out_weight.shape[1]
    half = tokens // 2
    blocks = tokens // BLK
    capacity = (R * blocks + shards - 1) // shards
    requests = blocks * R
    pairs = width // LANES
    sent_rows = 2 * capacity * BLK + 2 * SUMR
    back_rows = sent_rows + model // shards
    nsum = shards * SUMR
    total = (3 + R) * BLK + nsum
    params = pltpu.CompilerParams(vmem_limit_bytes=VMEM)

    wanted = partners.reshape(-1)
    owners = wanted // blocks
    inside = wanted % blocks
    order = jnp.arange(requests)
    earlier = (owners[:, None] == owners[None, :]) & (order[None, :] < order[:, None])
    ranks = jnp.sum(earlier.astype(jnp.int32), 1)
    slots = owners * capacity + ranks
    hits = (slots[:, None] == jnp.arange(shards * capacity)[None, :]).astype(jnp.int32)
    asks = (jnp.sum(hits * (inside[:, None] + 1), 0) - 1).reshape(shards, capacity)
    asked = lax.all_to_all(asks, "seq", split_axis=0, concat_axis=0, tiled=True).reshape(-1)
    weight_other = lax.ppermute(out_weight, "head", [(0, 1), (1, 0)])
    fillers = jnp.sum(hits * order[:, None], 0)
    meta = jnp.concatenate([slots, fillers])

    whole = pl.BlockSpec((tokens, width), lambda s, m: (0, 0))
    sent = pl.pallas_call(
        functools.partial(pack_kernel, capacity),
        out_shape=jax.ShapeDtypeStruct((pairs, shards, sent_rows, LANES), BF16),
        grid_spec=pltpu.PrefetchScalarGridSpec(
            num_scalar_prefetch=1,
            grid=(shards,),
            in_specs=[whole, whole],
            out_specs=pl.BlockSpec((pairs, 1, sent_rows, LANES), lambda s, m: (0, s, 0, 0)),
        ),
        compiler_params=params,
        name="pack",
    )(asked, keys, values)

    vmem = pl.BlockSpec(memory_space=pltpu.VMEM)
    anywhere = pl.BlockSpec(memory_space=pl.ANY)
    sems = pltpu.SemaphoreType.DMA
    mixed, grad_queries, dk, dv, returned, halo = pl.pallas_call(
        functools.partial(attend_kernel, shards, capacity),
        out_shape=[
            jax.ShapeDtypeStruct((half, model), BF16),
            jax.ShapeDtypeStruct((tokens, width), BF16),
            jax.ShapeDtypeStruct((tokens, width), F32),
            jax.ShapeDtypeStruct((tokens, width), F32),
            jax.ShapeDtypeStruct((pairs, shards, back_rows, LANES), BF16),
            jax.ShapeDtypeStruct((pairs, 2, 2 * BLK, LANES), BF16),
        ],
        in_specs=[pl.BlockSpec(memory_space=pltpu.SMEM), vmem, vmem, vmem]
        + [anywhere] * 4,
        out_specs=[vmem] * 4 + [anywhere] * 2,
        scratch_shapes=[
            pltpu.VMEM((tokens + 2 * BLK, width), BF16),
            pltpu.VMEM((tokens + 2 * BLK, width), BF16),
            pltpu.VMEM((tokens, model), BF16),
            pltpu.VMEM((tokens, width), BF16),
            pltpu.VMEM((pairs, tokens, LANES), BF16),
            pltpu.VMEM((pairs, half, LANES), BF16),
            pltpu.VMEM((pairs, shards, sent_rows, LANES), BF16),
            pltpu.VMEM((shards * capacity, BLK, LANES), BF16),
            pltpu.VMEM((shards * capacity, BLK, LANES), BF16),
            pltpu.VMEM((requests, BLK, LANES), BF16),
            pltpu.VMEM((requests, BLK, LANES), BF16),
            pltpu.VMEM((pairs, shards, back_rows, LANES), BF16),
            pltpu.VMEM((pairs, 2, 2 * BLK, LANES), BF16),
            pltpu.VMEM((total, LANES), BF16),
            pltpu.VMEM((total, LANES), BF16),
            pltpu.VMEM((tokens + 2 * BLK, LANES), F32),
            pltpu.VMEM((tokens + 2 * BLK, LANES), F32),
            pltpu.VMEM((nsum, LANES), F32),
            pltpu.VMEM((nsum, LANES), F32),
            sems((3,)), sems((4,)), sems((4,)), sems, sems,
            sems((pairs, shards)), sems((pairs, shards)),
            sems((pairs, shards)), sems((pairs, shards)),
            sems((pairs, 2)), sems((pairs, 2)), sems((pairs,)), sems((pairs,)),
        ],
        compiler_params=pltpu.CompilerParams(
            vmem_limit_bytes=VMEM, collective_id=0, has_side_effects=True
        ),
        name="attend",
    )(meta, queries, out_weight, weight_other, keys, values, grad_out, sent)

    local = lambda p, m: (0, p)
    local4 = lambda p, m: (p, 0, 0, 0)
    grad_keys, grad_values, grad_weight = pl.pallas_call(
        functools.partial(combine_kernel, capacity),
        out_shape=[
            jax.ShapeDtypeStruct((tokens, width), BF16),
            jax.ShapeDtypeStruct((tokens, width), BF16),
            jax.ShapeDtypeStruct((model // shards, width), F32),
        ],
        grid_spec=pltpu.PrefetchScalarGridSpec(
            num_scalar_prefetch=1,
            grid=(pairs,),
            in_specs=[
                pl.BlockSpec((tokens, LANES), local),
                pl.BlockSpec((tokens, LANES), local),
                pl.BlockSpec((1, 2, 2 * BLK, LANES), local4),
                pl.BlockSpec((1, shards, back_rows, LANES), local4),
            ],
            out_specs=[
                pl.BlockSpec((tokens, LANES), local),
                pl.BlockSpec((tokens, LANES), local),
                pl.BlockSpec((model // shards, LANES), local),
            ],
            scratch_shapes=[pltpu.VMEM((tokens, LANES), F32)],
        ),
        compiler_params=params,
        name="combine",
    )(asked, dk, dv, halo, returned)
    return (mixed, grad_queries, grad_keys, grad_values, grad_weight.T)


def solution(mesh):
    in_specs = (
        P("seq", "head"),
        P("seq", "head"),
        P("seq", "head"),
        P("seq", None),
        P("head", None),
        P(("seq", "head"), None),
    )
    out_specs = (
        P(("seq", "head"), None),
        P("seq", "head"),
        P("seq", "head"),
        P("seq", "head"),
        P("head", "seq"),
    )
    return jax.shard_map(
        per_device, mesh=mesh, in_specs=in_specs, out_specs=out_specs, check_vma=False
    )
```

time: 468 us -> 373 us (0.80)
  waiting for transfers between devices: 301 us -> 3.15 us
  Pallas kernels: 91.1 us -> 353 us
  starting transfers between devices: 25.5 us -> 8.14 us
  between operations: 14.3 us -> 0.69 us
  blocking collectives: 10.2 us -> 0 us
  local copies, waits for them, and re-layouts: 14 us -> 5.57 us
  matrix products: 7.86 us -> 0 us
    ppermute x6 -> x1, waiting for transfers between devices: 301 us -> 0.01 us  [per_device(): weight_other = lax.ppermute(out_weight, 'head', [(0, 1), (1, 0)])]
    pallas_call x2, Pallas kernels: 77.3 us -> 343 us  [the longest x1 334 us: per_device(): pl.pallas_call(functools.partial(attend_kernel, shards, capacity), out_sh...]
    ppermute x6 -> x1, starting transfers between devices: 13.3 us -> 1.3 us  [per_device(): weight_other = lax.ppermute(out_weight, 'head', [(0, 1), (1, 0)])]
    all_to_all x1 -> x0, blocking collectives: 10.2 us -> none  [per_device(): lax.all_to_all(asks, 'seq', split_axis=0, concat_axis=0, tiled=True)]
    unnamed x34 -> x9, local copies, waits for them, and re-layouts: 13.1 us -> 3.68 us
    dot_general x3 -> x0, matrix products: 7.86 us -> none  [the longest x1 4.22 us: per_device(): lax.dot_general(grad_full, out_weight, (((1,), (1,)), ((), ())), preferre...]
    all_to_all x2 -> x1, starting transfers between devices: 12.2 us -> 6.83 us  [per_device(): lax.all_to_all(asks, 'seq', split_axis=0, concat_axis=0, tiled=True)]
  transfers between devices with their start and end apart: 9 -> 2, of which waited for: 5 -> 1; matrix products, arithmetic and copies ran while one was open for 2% -> 1% of each run, Pallas kernels for 0% -> 3%
where the time goes in v2:
time: 373 us; the launch traced here: 372 us
  Pallas kernels  353 us (95%)
  starting transfers between devices  8.14 us (2%)
  local copies, waits for them, and re-layouts  5.57 us (1%)
    pallas_call x1, Pallas kernels, per_device(): pl.pallas_call(functools.partial(attend_kernel, shards, capacity), out_sh...  334 us
    pallas_call x1, Pallas kernels, per_device(): pl.pallas_call(functools.partial(combine_kernel, capacity), out_shape=[ja...  10 us
    pallas_call x1, Pallas kernels, per_device(): pl.pallas_call(functools.partial(pack_kernel, capacity), out_shape=jax.Sh...  9.53 us
  transfers between devices with their start and end apart: 2, of which 1 were waited for; matrix products, arithmetic and copies ran while one was open for 1% of the time, Pallas kernels for 3%

profile of v2, /device:TPU:11, one launch (start us, length us, event | category | flops | bytes accessed | tf_op | source)
XLA Modules:
  0.0 372.5 jit_solution(9976104208931402295)
XLA Ops:
  0.6 1.3 collective-permute-start
  1.9 0.8 copy.15
  2.7 0.1 reshape.125
  2.8 0.2 convert_reduce_fusion
  3.0 0.1 select_reduce_fusion
  3.1 0.7 sub.14
  3.8 6.8 %all-to-all-start = ((s32[16,1,3]{2,1,0:T(1,128)}), s32[16,1,3]{2,1,0:T(1,128)S(1)}, u32[]{:S(2)}, u32[]{:S(2)}) async-start(s32[16,1,3]{2,1,0:T(1,128)} %bitcast), calls=%async_computation | async-start | bytes 16384 | tf_op jit(solution)/shard_map/all_to_all | solution.py:368
  10.6 0.6 pad_add_fusion.meta
  11.2 3.1 all-to-all-done
  14.4 0.5 broadcast.147
  14.9 0.7 reduce.3
  15.5 0.6 reshape.126.asked
  16.1 9.5 %pack.1.sent = bf16[4,16,416,128]{3,2,1,0:T(8,128)(2,1)} custom-call(s32[48]{0:T(128)} %reshape.126.asked, bf16[1024,512]{1,0:T(8,128)(2,1)} %k_hbm.1, bf16[1024,512]{1,0:T(8,128)(2,1)} %v_hbm.1), custom_call_target="tpu_custom_call" | custom-call | tf_op jit(solution)/shard_map/pack/pallas_call | solution.py:374
  25.7 0.0 collective-permute-done.wo_ref
  25.7 0.0 copy-start
  25.7 1.0 copy-done
  26.6 333.9 %attend.1 = (bf16[512,1024]{1,0:T(8,128)(2,1)}, bf16[1024,512]{1,0:T(8,128)(2,1)}, f32[1024,512]{1,0:T(8,128)}, f32[1024,512]{1,0:T(8,128)}, bf16[4,16,480,128]{...) custom-call(s32[96]{0:T(128)} %pad_add_fusion.meta, bf16[1024,512]{1,0:T(8,128)(2,1)} %q_ref.1, bf16[512,1024]{1,0:T(8,128)(2,1)} %w_ref.1, ...), custom_call_target="tpu_custom_call" | custom-call | tf_op jit(solution)/shard_map/attend/pallas_call | solution.py:390
  360.5 0.0 copy-start.2
  360.5 0.0 copy-start.1
  360.5 10.0 %combine.1 = (bf16[1024,512]{1,0:T(8,128)(2,1)}, bf16[1024,512]{1,0:T(8,128)(2,1)}, f32[64,512]{1,0:T(8,128)}) custom-call(s32[48]{0:T(128)} %reshape.126.asked, f32[1024,512]{1,0:T(8,128)} %get-tuple-element.16.dk_ref, f32[1024,512]{1,0:T(8,128)} %get-tuple-element.17.dv_ref, bf16[4,2,128,128]{3,2,1,0:T(8,128)(2,1)} %get-tuple-element.18.halo, ...), custom_call_target="tpu_custom_call" | custom-call | tf_op jit(solution)/shard_map/combine/pallas_call | solution.py:436
  370.5 0.0 copy-done.2
  370.5 1.0 copy.19
  371.5 0.0 copy-done.1
  371.5 1.0 copy.20
  (3 shorter events, 0.0 us)
Async XLA Ops:
  0.6 25.0 %collective-permute-start = (bf16[512,1024]{1,0:T(8,128)(2,1)}, bf16[512,1024]{1,0:T(8,128)(2,1)S(1)}, u32[]{:S(2)}, u32[]{:S(2)}) collective-permute-start(bf16[512,1024]{1,0:T(8,128)(2,1)} %w_ref.1), channel_id=1, source_target_pairs={{0,1},{1,0},{2,3},{3,2},{4,5},{5,4},{6,7},{7,6},{8,9},{9,8},{10,11... | collective-permute-start | bytes 3145736 | tf_op jit(solution)/shard_map/ppermute | solution.py:369
  3.8 10.6 %all-to-all-start = ((s32[16,1,3]{2,1,0:T(1,128)}), s32[16,1,3]{2,1,0:T(1,128)S(1)}, u32[]{:S(2)}, u32[]{:S(2)}) async-start(s32[16,1,3]{2,1,0:T(1,128)} %bitcast), calls=%async_computation | async-start | bytes 16384 | tf_op jit(solution)/shard_map/all_to_all | solution.py:368
  25.7 1.0 copy-start
  360.5 10.0 %copy-start.2 = (bf16[512,1024]{1,0:T(8,128)(2,1)S(1)}, bf16[512,1024]{1,0:T(8,128)(2,1)}, u32[]{:S(2)}) copy-start(bf16[512,1024]{1,0:T(8,128)(2,1)} %get-tuple-element.32) | copy-start | bytes 3145732
  360.5 11.0 %copy-start.1 = (bf16[1024,512]{1,0:T(8,128)(2,1)S(1)}, bf16[1024,512]{1,0:T(8,128)(2,1)}, u32[]{:S(2)}) copy-start(bf16[1024,512]{1,0:T(8,128)(2,1)} %get-tuple-element.33) | copy-start | bytes 3145732

commit v3 on v2

--- a/solution.py
+++ b/solution.py
@@ -11,6 +11,7 @@
 BLK = 64
 R = 3
 SUMR = 16
+GROUP = 4
 LANES = 128
 VMEM = 58 * 1024 * 1024
 F32 = jnp.float32
@@ -36,11 +37,13 @@
 def attend_kernel(
     shards, capacity,
     meta, q_ref, w_ref, wo_ref, k_hbm, v_hbm, go_hbm, sent,
-    mixed_ref, dq_ref, dk_ref, dv_ref, returned, halo_in,
+    mixed_ref, dq_ref, dk_ref, dv_ref, returned, halo_in, terms_in,
     kpad, vpad, gf, g_all, att, received, arrived, cur_k, cur_v, part_k, part_v, back, halo_out,
+    terms, group_in, group_sum,
     kl, vl, dka, dva, dks, dvs,
     local_sem, halo_send, halo_recv, go_send, go_recv, out_send, out_recv,
     ret_send, ret_recv, edge_send, edge_recv, att_send, att_recv,
+    group_send, group_recv, terms_send, terms_recv,
 ):
     tokens, width = q_ref.shape
     model = w_ref.shape[1]
@@ -55,6 +58,9 @@
     weight_at = sum_at + 2 * SUMR
     weight_rows = model // shards
     me = lax.axis_index("seq")
+    groups = shards // GROUP
+    group = me // GROUP
+    seat = lax.rem(me, GROUP)
     side = lax.axis_index("head")
     after = lax.rem(me + 1, shards)
     before = lax.rem(me + shards - 1, shards)
@@ -149,6 +155,31 @@
     def att_copy(c):
         return remote(att.at[c, other_rows], received.at[c], att_send.at[c], att_recv.at[c],
                       {"head": other})
+
+    def group_copy(c, k):
+        mate = lax.rem(seat + k, GROUP)
+        return remote(terms.at[c, mate], group_in.at[c, seat], group_send.at[c, k],
+                      group_recv.at[c, k], {"seq": group * GROUP + mate})
+
+    def group_arrival(c, k):
+        mate = lax.rem(seat + GROUP - k, GROUP)
+        return remote(terms.at[c, mate], group_in.at[c, mate], group_send.at[c, k],
+                      group_recv.at[c, k], {"seq": group * GROUP + mate})
+
+    def terms_copy(c, k):
+        there = lax.rem(group + k, groups)
+        return remote(group_sum.at[c, there], terms_in.at[c, group], terms_send.at[c, k],
+                      terms_recv.at[c, k], {"seq": there * GROUP + seat})
+
+    def terms_arrival(c, k):
+        there = lax.rem(group + groups - k, groups)
+        return remote(group_sum.at[c, there], terms_in.at[c, there], terms_send.at[c, k],
+                      terms_recv.at[c, k], {"seq": there * GROUP + seat})
+
+    def own_terms(c):
+        return pltpu.make_async_copy(
+            group_sum.at[c, group], terms_in.at[c, group], terms_recv.at[c, 0]
+        )
 
     def pair(c, carry):
         cols = pl.ds(pl.multiple_of(c * LANES, LANES), LANES)
@@ -224,6 +255,24 @@
         lax.fori_loop(0, blocks, step, 0)
         att_copy(c).start()
 
+        for n, ref in enumerate((dks, dvs)):
+            sums = ref[...].astype(BF16).reshape(groups, GROUP, SUMR, LANES)
+            for q in range(GROUP):
+                terms[c, q, :, n * SUMR : (n + 1) * SUMR, :] = sums[:, q]
+        count = 256 // (weight_rows * GROUP)
+
+        def weigh(j, carry):
+            columns = pl.ds(pl.multiple_of(j * 256, 256), 256)
+            product = lax.dot_general(gf[:, columns], att[c], tn, preferred_element_type=F32)
+            product = product.astype(BF16).reshape(count, GROUP, weight_rows, LANES)
+            for q in range(GROUP):
+                terms[c, q, pl.ds(j * count, count), 2 * SUMR :, :] = product[:, q]
+            return carry
+
+        lax.fori_loop(0, model // 256, weigh, 0)
+        for k in range(1, GROUP):
+            group_copy(c, k).start()
+
         def fill(d, carry):
             for n in range(capacity):
                 request = meta[requests + d * capacity + n]
@@ -234,23 +283,6 @@
             return carry
 
         lax.fori_loop(0, shards, fill, 0)
-        back[c, :, sum_at : sum_at + SUMR, :] = (
-            dks[...].astype(BF16).reshape(shards, SUMR, LANES)
-        )
-        back[c, :, sum_at + SUMR : weight_at, :] = (
-            dvs[...].astype(BF16).reshape(shards, SUMR, LANES)
-        )
-        count = 256 // weight_rows
-
-        def weigh(j, carry):
-            columns = pl.ds(pl.multiple_of(j * 256, 256), 256)
-            terms = lax.dot_general(gf[:, columns], att[c], tn, preferred_element_type=F32)
-            back[c, pl.ds(j * count, count), weight_at:, :] = terms.astype(BF16).reshape(
-                count, weight_rows, LANES
-            )
-            return carry
-
-        lax.fori_loop(0, model // 256, weigh, 0)
 
         def send(k, carry):
             to = lax.rem(me + k, shards)
@@ -272,6 +304,29 @@
 
     lax.fori_loop(0, pairs, pair, 0)
 
+    def add_up(c, carry):
+        for k in range(1, GROUP):
+            group_arrival(c, k).wait_recv()
+
+        def add(z, carry):
+            value = terms[c, seat, z].astype(F32)
+            for k in range(1, GROUP):
+                value = value + group_in[c, lax.rem(seat + k, GROUP), z].astype(F32)
+            group_sum[c, z] = value.astype(BF16)
+            return carry
+
+        lax.fori_loop(0, groups, add, 0)
+
+        def send(k, carry):
+            terms_copy(c, k).start()
+            return carry
+
+        lax.fori_loop(1, groups, send, 0)
+        own_terms(c).start()
+        return carry
+
+    lax.fori_loop(0, pairs, add_up, 0)
+
     def swapped(c, carry):
         att_copy(c).wait()
         return carry
@@ -306,23 +361,31 @@
         pltpu.make_async_copy(back.at[c, me], returned.at[c, me], ret_recv.at[c, 0]).wait()
         for copy in edge_copies(c):
             copy.wait()
+        for k in range(1, GROUP):
+            group_copy(c, k).wait_send()
+
+        def summed(k, carry):
+            terms_copy(c, k).wait_send()
+            terms_arrival(c, k).wait_recv()
+            return carry
+
+        lax.fori_loop(1, groups, summed, 0)
+        own_terms(c).wait()
         return carry
 
     lax.fori_loop(0, pairs, finish, 0)
 
 
-def combine_kernel(capacity, asked, dk_ref, dv_ref, halo, back, gk_ref, gv_ref, gw_ref, acc):
+def combine_kernel(capacity, asked, dk_ref, dv_ref, halo, back, terms, gk_ref, gv_ref, gw_ref, acc):
     shards = back.shape[1]
     tokens = gk_ref.shape[0]
-    sum_at = 2 * capacity * BLK
-    weight_at = sum_at + 2 * SUMR
     for j, (own, out) in enumerate(((dk_ref, gk_ref), (dv_ref, gv_ref))):
         acc[...] = own[...]
         side = slice(j * BLK, (j + 1) * BLK)
         acc[:BLK, :] += halo[0, 0, side, :].astype(F32)
         acc[tokens - BLK :, :] += halo[0, 1, side, :].astype(F32)
-        at = sum_at + j * SUMR
-        acc[:SUMR, :] += jnp.sum(back[0, :, at : at + SUMR, :].astype(F32), 0)
+        at = j * SUMR
+        acc[:SUMR, :] += jnp.sum(terms[0, :, at : at + SUMR, :].astype(F32), 0)
 
         def add(shard, carry):
             for n in range(capacity):
@@ -338,7 +401,7 @@
 
         lax.fori_loop(0, shards, add, 0)
         out[...] = acc[...].astype(BF16)
-    gw_ref[...] = jnp.sum(back[0, :, weight_at:, :].astype(F32), 0)
+    gw_ref[...] = jnp.sum(terms[0, :, 2 * SUMR :, :].astype(F32), 0)
 
 
 def per_device(queries, keys, values, partners, out_weight, grad_out):
@@ -351,7 +414,9 @@
     requests = blocks * R
     pairs = width // LANES
     sent_rows = 2 * capacity * BLK + 2 * SUMR
-    back_rows = sent_rows + model // shards
+    back_rows = 2 * capacity * BLK
+    groups = shards // GROUP
+    term_rows = 2 * SUMR + model // shards
     nsum = shards * SUMR
     total = (3 + R) * BLK + nsum
     params = pltpu.CompilerParams(vmem_limit_bytes=VMEM)
@@ -387,7 +452,7 @@
     vmem = pl.BlockSpec(memory_space=pltpu.VMEM)
     anywhere = pl.BlockSpec(memory_space=pl.ANY)
     sems = pltpu.SemaphoreType.DMA
-    mixed, grad_queries, dk, dv, returned, halo = pl.pallas_call(
+    mixed, grad_queries, dk, dv, returned, halo, terms = pl.pallas_call(
         functools.partial(attend_kernel, shards, capacity),
         out_shape=[
             jax.ShapeDtypeStruct((half, model), BF16),
@@ -396,10 +461,11 @@
             jax.ShapeDtypeStruct((tokens, width), F32),
             jax.ShapeDtypeStruct((pairs, shards, back_rows, LANES), BF16),
             jax.ShapeDtypeStruct((pairs, 2, 2 * BLK, LANES), BF16),
+            jax.ShapeDtypeStruct((pairs, groups, term_rows, LANES), BF16),
         ],
         in_specs=[pl.BlockSpec(memory_space=pltpu.SMEM), vmem, vmem, vmem]
         + [anywhere] * 4,
-        out_specs=[vmem] * 4 + [anywhere] * 2,
+        out_specs=[vmem] * 4 + [anywhere] * 3,
         scratch_shapes=[
             pltpu.VMEM((tokens + 2 * BLK, width), BF16),
             pltpu.VMEM((tokens + 2 * BLK, width), BF16),
@@ -414,6 +480,9 @@
             pltpu.VMEM((requests, BLK, LANES), BF16),
             pltpu.VMEM((pairs, shards, back_rows, LANES), BF16),
             pltpu.VMEM((pairs, 2, 2 * BLK, LANES), BF16),
+            pltpu.VMEM((pairs, GROUP, groups, term_rows, LANES), BF16),
+            pltpu.VMEM((pairs, GROUP, groups, term_rows, LANES), BF16),
+            pltpu.VMEM((pairs, groups, term_rows, LANES), BF16),
             pltpu.VMEM((total, LANES), BF16),
             pltpu.VMEM((total, LANES), BF16),
             pltpu.VMEM((tokens + 2 * BLK, LANES), F32),
@@ -424,6 +493,8 @@
             sems((pairs, shards)), sems((pairs, shards)),
             sems((pairs, shards)), sems((pairs, shards)),
             sems((pairs, 2)), sems((pairs, 2)), sems((pairs,)), sems((pairs,)),
+            sems((pairs, GROUP)), sems((pairs, GROUP)),
+            sems((pairs, groups)), sems((pairs, groups)),
         ],
         compiler_params=pltpu.CompilerParams(
             vmem_limit_bytes=VMEM, collective_id=0, has_side_effects=True
@@ -448,6 +519,7 @@
                 pl.BlockSpec((tokens, LANES), local),
                 pl.BlockSpec((1, 2, 2 * BLK, LANES), local4),
                 pl.BlockSpec((1, shards, back_rows, LANES), local4),
+                pl.BlockSpec((1, groups, term_rows, LANES), local4),
             ],
             out_specs=[
                 pl.BlockSpec((tokens, LANES), local),
@@ -458,7 +530,7 @@
         ),
         compiler_params=params,
         name="combine",
-    )(asked, dk, dv, halo, returned)
+    )(asked, dk, dv, halo, returned, terms)
     return (mixed, grad_queries, grad_keys, grad_values, grad_weight.T)
 
 

time: 373 us -> 346 us (0.928)
  Pallas kernels: 353 us -> 325 us
    pallas_call x1, Pallas kernels: 334 us -> 306 us  [per_device(): pl.pallas_call(functools.partial(attend_kernel, shards, capacity), out_sh...]
where the time goes in v3:
time: 346 us; the launch traced here: 344 us
  Pallas kernels  325 us (94%)
  starting transfers between devices  8.14 us (2%)
  local copies, waits for them, and re-layouts  5.57 us (2%)
    pallas_call x1, Pallas kernels, per_device(): pl.pallas_call(functools.partial(attend_kernel, shards, capacity), out_sh...  306 us
    pallas_call x1, Pallas kernels, per_device(): pl.pallas_call(functools.partial(combine_kernel, capacity), out_shape=[ja...  9.52 us
    pallas_call x1, Pallas kernels, per_device(): pl.pallas_call(functools.partial(pack_kernel, capacity), out_shape=jax.Sh...  9.42 us
  transfers between devices with their start and end apart: 2, of which 1 were waited for; matrix products, arithmetic and copies ran while one was open for 1% of the time, Pallas kernels for 3%

profile of v3, /device:TPU:11, one launch (start us, length us, event | category | flops | bytes accessed | tf_op | source)
XLA Modules:
  0.0 344.4 jit_solution(13762737431553589873)
XLA Ops:
  0.6 1.3 collective-permute-start
  1.9 0.8 copy.15
  2.7 0.1 reshape.125
  2.8 0.2 convert_reduce_fusion
  3.0 0.1 select_reduce_fusion
  3.1 0.7 sub.14
  3.8 6.8 %all-to-all-start = ((s32[16,1,3]{2,1,0:T(1,128)}), s32[16,1,3]{2,1,0:T(1,128)S(1)}, u32[]{:S(2)}, u32[]{:S(2)}) async-start(s32[16,1,3]{2,1,0:T(1,128)} %bitcast), calls=%async_computation | async-start | bytes 16384 | tf_op jit(solution)/shard_map/all_to_all | solution.py:433
  10.6 0.6 pad_add_fusion.meta
  11.2 3.1 all-to-all-done
  14.4 0.5 broadcast.147
  14.9 0.7 reduce.3
  15.5 0.6 reshape.126.asked
  16.1 9.4 %pack.1.sent = bf16[4,16,416,128]{3,2,1,0:T(8,128)(2,1)} custom-call(s32[48]{0:T(128)} %reshape.126.asked, bf16[1024,512]{1,0:T(8,128)(2,1)} %k_hbm.1, bf16[1024,512]{1,0:T(8,128)(2,1)} %v_hbm.1), custom_call_target="tpu_custom_call" | custom-call | tf_op jit(solution)/shard_map/pack/pallas_call | solution.py:439
  25.6 0.0 collective-permute-done.wo_ref
  25.6 0.0 copy-start
  25.6 1.0 copy-done
  26.5 306.4 %attend.1 = (bf16[512,1024]{1,0:T(8,128)(2,1)}, bf16[1024,512]{1,0:T(8,128)(2,1)}, f32[1024,512]{1,0:T(8,128)}, f32[1024,512]{1,0:T(8,128)}, bf16[4,16,384,128]{...) custom-call(s32[96]{0:T(128)} %pad_add_fusion.meta, bf16[1024,512]{1,0:T(8,128)(2,1)} %q_ref.1, ...), custom_call_target="tpu_custom_call" | custom-call | tf_op jit(solution)/shard_map/attend/pallas_call | solution.py:455
  332.9 0.0 copy-start.2
  333.0 0.0 copy-start.1
  333.0 9.5 %combine.1 = (bf16[1024,512]{1,0:T(8,128)(2,1)}, bf16[1024,512]{1,0:T(8,128)(2,1)}, f32[64,512]{1,0:T(8,128)}) custom-call(s32[48]{0:T(128)} %reshape.126.asked, f32[1024,512]{1,0:T(8,128)} %get-tuple-element.17.dk_ref, f32[1024,512]{1,0:T(8,128)} %get-tuple-element.18.dv_ref, bf16[4,2,128,128]{3,2,1,0:T(8,128)(2,1)} %get-tuple-element.19.halo, ...), custom_call_target="tpu_custom_call" | custom-call | tf_op jit(solution)/shard_map/combine/pallas_call | solution.py:507
  342.5 0.0 copy-done.2
  342.5 1.0 copy.19
  343.5 0.0 copy-done.1
  343.5 1.0 copy.20
  (3 shorter events, 0.0 us)
Async XLA Ops:
  0.6 24.9 %collective-permute-start = (bf16[512,1024]{1,0:T(8,128)(2,1)}, bf16[512,1024]{1,0:T(8,128)(2,1)S(1)}, u32[]{:S(2)}, u32[]{:S(2)}) collective-permute-start(bf16[512,1024]{1,0:T(8,128)(2,1)} %w_ref.1), channel_id=1, source_target_pairs={{0,1},{1,0},{2,3},{3,2},{4,5},{5,4},{6,7},{7,6},{8,9},{9,8},{10,11... | collective-permute-start | bytes 3145736 | tf_op jit(solution)/shard_map/ppermute | solution.py:434
  3.8 10.6 %all-to-all-start = ((s32[16,1,3]{2,1,0:T(1,128)}), s32[16,1,3]{2,1,0:T(1,128)S(1)}, u32[]{:S(2)}, u32[]{:S(2)}) async-start(s32[16,1,3]{2,1,0:T(1,128)} %bitcast), calls=%async_computation | async-start | bytes 16384 | tf_op jit(solution)/shard_map/all_to_all | solution.py:433
  25.6 1.0 copy-start
  332.9 9.5 %copy-start.2 = (bf16[512,1024]{1,0:T(8,128)(2,1)S(1)}, bf16[512,1024]{1,0:T(8,128)(2,1)}, u32[]{:S(2)}) copy-start(bf16[512,1024]{1,0:T(8,128)(2,1)} %get-tuple-element.34) | copy-start | bytes 3145732
  333.0 10.5 %copy-start.1 = (bf16[1024,512]{1,0:T(8,128)(2,1)S(1)}, bf16[1024,512]{1,0:T(8,128)(2,1)}, u32[]{:S(2)}) copy-start(bf16[1024,512]{1,0:T(8,128)(2,1)} %get-tuple-element.35) | copy-start | bytes 3145732
